TPU v7x, 512 devices: a whole 4x8x8 slice. The times are simulated.
512 devices in a mesh: dp: 16 (over y, core), ctx: 32 (over z, x).
Axes of the slice: x: 4, y: 8, z: 8, core: 2. Of those that a mesh axis runs over, the one named last changes fastest.
Arguments:
- query_rows: bfloat16 [65536, 4096], P(('dp', 'ctx')), may hold values from -108 to 108
- rotated_key_rows: bfloat16 [65536, 1024], P(('dp', 'ctx')), may hold values from -4 to 4
- value_head_rows: bfloat16 [65536, 1024], P(('dp', 'ctx')), may hold values from -6 to 6
- doc_lengths: int32 [16, 1, 8], P('dp'), may hold values from 1 to 2048, 4096 in all within a row
- send_slot_index: int32 [16, 32, 192], P('dp', 'ctx'), may hold values from 0 to 128, as said below
- slab_source_index: int32 [16, 32, 128], P('dp', 'ctx'), may hold values from 0 to 191, as said below
- back_pack: int32 [16, 32, 192], P('dp', 'ctx'), may hold values from 0 to 128, as said below
- back_index: int32 [16, 32, 128], P('dp', 'ctx'), may hold values from 0 to 191, as said below
Outputs:
- attention_out: bfloat16 [65536, 4096], P(('dp', 'ctx'))
Inputs may be any that keep to these rules, and one draw needn't show every extreme that they name: `send_slot_index`: in each slab every row 0 to 127 appears once; slot block j (slots j * 12 onward) holds the rows sent to slab (j, c), used slots first and 128 in the others; at most 12 rows go from one slab to one slab, and some slab sends exactly 12. `slab_source_index`: names every used received slot of the slab once, as source times 12 plus slot. `back_pack`: sends every placed row back to the slab and slot it came from: entries 128 mark the slots that send_slot_index left empty. `back_index`: names for every row the slot in which it returns.
All inputs are finite; a program needn't handle non-finite values.
Results may differ from a plain program's by a relative error of at most 0.0036.
Values may be sent and summed in bfloat16 or wider, within the bound.
No kernel may reach another device: no remote copies, remote signals or barrier semaphores. Data moves between devices by JAX's collectives and lax.ppermute only.
A program may use at most 128 MiB of HBM per device.

v0:
```python
import math

import jax
import jax.numpy as jnp
from jax import lax
from jax.sharding import PartitionSpec as P

QUERY_HEADS = 32
KEY_VALUE_HEADS = 8
HEAD_SIZE = 128
PACKS = 1


def document_ids(lengths, pack_rows):
    bounds = jnp.cumsum(lengths)
    places = jnp.arange(pack_rows, dtype=jnp.int32)
    return jnp.sum((places[:, None] >= bounds[None, :]).astype(jnp.int32), axis=1)


def fill_slots(source, slot_table):
    padded = jnp.concatenate([source, jnp.zeros((1, source.shape[1]), source.dtype)], axis=0)
    return jnp.take(padded, slot_table, axis=0)


def attend(head_q, key_per_head, value_per_head, doc_ids):
    pack_rows = head_q.shape[0]
    score_scale = 1.0 / math.sqrt(head_q.shape[2])
    tile_rows = min(512, pack_rows)
    outputs = []
    for block_index in range(pack_rows // tile_rows):
        start_row = block_index * tile_rows
        end_row = start_row + tile_rows
        block_q = head_q[start_row:end_row]
        scores = (
            jnp.einsum(
                "qhe,khe->hqk", block_q, key_per_head[:end_row], preferred_element_type=jnp.float32
            )
            * score_scale
        )
        query_at = start_row + jnp.arange(tile_rows, dtype=jnp.int32)
        key_at = jnp.arange(end_row, dtype=jnp.int32)
        allowed = (doc_ids[start_row:end_row][:, None] == doc_ids[:end_row][None, :]) & (
            key_at[None, :] <= query_at[:, None]
        )
        scores = jnp.where(allowed[None], scores, -jnp.inf)
        row_max = jnp.max(scores, axis=2, keepdims=True)
        weights = jnp.exp(scores - row_max)
        totals = jnp.sum(weights, axis=2)
        probabilities = weights.astype(jnp.bfloat16)
        weighted = jnp.einsum(
            "hqk,khe->qhe",
            probabilities,
            value_per_head[:end_row],
            preferred_element_type=jnp.float32,
        )
        outputs.append((weighted / jnp.transpose(totals)[:, :, None]).astype(jnp.bfloat16))
    return jnp.concatenate(outputs, axis=0)


def local(
    query_rows,
    rotated_key_rows,
    value_head_rows,
    doc_lengths,
    send_slot_index,
    slab_source_index,
    back_pack,
    back_index,
):
    rows_per_slab = query_rows.shape[0]
    widen_heads = QUERY_HEADS // KEY_VALUE_HEADS
    send_table = send_slot_index[0, 0]
    lookup_table = slab_source_index[0, 0]
    group_rows = rows_per_slab * lax.axis_size("ctx")
    pack_rows = group_rows // PACKS
    moved_q, shipped_keys, shipped_values = (
        lax.all_to_all(
            fill_slots(query_rows, send_table), "dp", split_axis=0, concat_axis=0, tiled=True
        ),
        lax.all_to_all(
            fill_slots(rotated_key_rows, send_table), "dp", split_axis=0, concat_axis=0, tiled=True
        ),
        lax.all_to_all(
            fill_slots(value_head_rows, send_table), "dp", split_axis=0, concat_axis=0, tiled=True
        ),
    )
    local_q = jnp.take(moved_q, lookup_table, axis=0).reshape(rows_per_slab, QUERY_HEADS, HEAD_SIZE)
    local_k = jnp.repeat(
        jnp.take(shipped_keys, lookup_table, axis=0).reshape(
            rows_per_slab, KEY_VALUE_HEADS, HEAD_SIZE
        ),
        widen_heads,
        axis=1,
    )
    local_v = jnp.repeat(
        jnp.take(shipped_values, lookup_table, axis=0).reshape(
            rows_per_slab, KEY_VALUE_HEADS, HEAD_SIZE
        ),
        widen_heads,
        axis=1,
    )
    head_q, key_per_head, value_per_head = (
        lax.all_to_all(local_q, "ctx", split_axis=1, concat_axis=0, tiled=True),
        lax.all_to_all(local_k, "ctx", split_axis=1, concat_axis=0, tiled=True),
        lax.all_to_all(local_v, "ctx", split_axis=1, concat_axis=0, tiled=True),
    )
    doc_ids = document_ids(doc_lengths[0, 0], pack_rows)
    pack_outputs = attend(head_q, key_per_head, value_per_head, doc_ids)
    slab_out = lax.all_to_all(pack_outputs, "ctx", split_axis=0, concat_axis=1, tiled=True)
    flat_out = slab_out.reshape(rows_per_slab, QUERY_HEADS * HEAD_SIZE)
    arrived = lax.all_to_all(
        fill_slots(flat_out, back_pack[0, 0]), "dp", split_axis=0, concat_axis=0, tiled=True
    )
    return jnp.take(arrived, back_index[0, 0], axis=0)


def solution(mesh):
    return jax.shard_map(
        local,
        mesh=mesh,
        in_specs=(
            P(("dp", "ctx"), None),
            P(("dp", "ctx"), None),
            P(("dp", "ctx"), None),
            P("dp", None, None),
            P("dp", "ctx", None),
            P("dp", "ctx", None),
            P("dp", "ctx", None),
            P("dp", "ctx", None),
        ),
        out_specs=P(("dp", "ctx"), None),
        check_vma=False,
    )
```

profile of v0, /device:TPU:1, one launch (start us, length us, event | category | flops | bytes accessed | tf_op | source)
XLA Modules:
  0.0 362.8 jit_solution(2474872866263952279)
XLA Ops:
  7.7 10.2 %all-to-all-start.4 = ((bf16[16,12,1024]{2,1,0:T(8,128)(2,1)}), bf16[16,12,1024]{2,1,0:T(8,128)(2,1)S(1)}, u32[]{:S(2)}, u32[]{:S(2)}) async-start(bf16[16,12,1024]{2,1,0:T(8,128)(2,1)} %all_to_all.88), calls=%async_computation.4 | async-start | bytes 1048576 | tf_op jit(solution)/shard_map/all_to_all | solution.py:80
  18.8 16.4 %all-to-all-done.4 = bf16[16,12,1024]{2,1,0:T(8,128)(2,1)S(1)} async-done(((bf16[16,12,1024]{2,1,0:T(8,128)(2,1)}), bf16[16,12,1024]{2,1,0:T(8,128)(2,1)S(1)}, u32[]{:S(2)}, u32[]{:S(2)}) %all-to-all-start.4) | async-done | bytes 393248 | tf_op jit(solution)/shard_map/all_to_all | solution.py:80
  35.2 3.5 all-to-all-start
  39.7 15.7 %all-to-all-done = bf16[16,12,1024]{2,1,0:T(8,128)(2,1)S(1)} async-done(((bf16[16,12,1024]{2,1,0:T(8,128)(2,1)}), bf16[16,12,1024]{2,1,0:T(8,128)(2,1)S(1)}, u32[]{:S(2)}, u32[]{:S(2)}) %all-to-all-start) | async-done | bytes 393248 | tf_op jit(solution)/shard_map/all_to_all | solution.py:83
  58.5 11.2 %all-to-all-start.5 = ((bf16[128,32,128]{2,0,1:T(8,128)(2,1)}), bf16[128,32,128]{2,0,1:T(8,128)(2,1)S(1)}, u32[]{:S(2)}, u32[]{:S(2)}) async-start(bf16[128,32,128]{2,0,1:T(8,128)(2,1)} %bitcast.13), calls=%async_computation.5 | async-start | bytes 2097152 | tf_op jit(solution)/shard_map/all_to_all | solution.py:104
  69.8 2.7 gather_fusion.2
  75.7 22.0 %all-to-all-done.5 = bf16[128,32,128]{2,0,1:T(8,128)(2,1)S(1)} async-done(((bf16[128,32,128]{2,0,1:T(8,128)(2,1)}), bf16[128,32,128]{2,0,1:T(8,128)(2,1)S(1)}, u32[]{:S(2)}, u32[]{:S(2)}) %all-to-all-start.5) | async-done | bytes 1048608 | tf_op jit(solution)/shard_map/all_to_all | solution.py:104
  97.7 3.9 %all-to-all-start.2 = ((bf16[16,12,4096]{2,1,0:T(8,128)(2,1)}), bf16[16,12,4096]{2,1,0:T(8,128)(2,1)S(1)}, u32[]{:S(2)}, u32[]{:S(2)}) async-start(bf16[16,12,4096]{2,1,0:T(8,128)(2,1)} %all_to_all.82), calls=%async_computation.2 | async-start | bytes 4194304 | tf_op jit(solution)/shard_map/all_to_all | solution.py:77
  102.6 48.0 %all-to-all-done.2 = bf16[16,12,4096]{2,1,0:T(8,128)(2,1)S(1)} async-done(((bf16[16,12,4096]{2,1,0:T(8,128)(2,1)}), bf16[16,12,4096]{2,1,0:T(8,128)(2,1)S(1)}, u32[]{:S(2)}, u32[]{:S(2)}) %all-to-all-start.2) | async-done | bytes 1572896 | tf_op jit(solution)/shard_map/all_to_all | solution.py:77
  152.2 5.0 %all-to-all-start.1 = ((bf16[128,32,128]{2,0,1:T(8,128)(2,1)}), bf16[128,32,128]{2,0,1:T(8,128)(2,1)S(1)}, u32[]{:S(2)}, u32[]{:S(2)}) async-start(bf16[128,32,128]{2,0,1:T(8,128)(2,1)} %bitcast.229), calls=%async_computation.1 | async-start | bytes 2097152 | tf_op jit(solution)/shard_map/all_to_all | solution.py:105
  157.3 2.5 all_to_all.84
  161.9 2.7 copy_bitcast_fusion.1
  164.6 19.0 %all-to-all-done.1 = bf16[128,32,128]{2,0,1:T(8,128)(2,1)S(1)} async-done(((bf16[128,32,128]{2,0,1:T(8,128)(2,1)}), bf16[128,32,128]{2,0,1:T(8,128)(2,1)S(1)}, u32[]{:S(2)}, u32[]{:S(2)}) %all-to-all-start.1) | async-done | bytes 1048608 | tf_op jit(solution)/shard_map/all_to_all | solution.py:105
  183.5 6.8 %all-to-all-start.3 = ((bf16[128,32,128]{2,0,1:T(8,128)(2,1)}), bf16[128,32,128]{2,0,1:T(8,128)(2,1)S(1)}, u32[]{:S(2)}, u32[]{:S(2)}) async-start(bf16[128,32,128]{2,0,1:T(8,128)(2,1)} %copy_bitcast_fusion.1), calls=%async_computation.3 | async-start | bytes 2097152 | tf_op jit(solution)/shard_map/all_to_all | solution.py:103
  205.8 10.0 %all-to-all-done.3 = bf16[128,32,128]{2,0,1:T(8,128)(2,1)S(1)} async-done(((bf16[128,32,128]{2,0,1:T(8,128)(2,1)}), bf16[128,32,128]{2,0,1:T(8,128)(2,1)S(1)}, u32[]{:S(2)}, u32[]{:S(2)}) %all-to-all-start.3) | async-done | bytes 1048608 | tf_op jit(solution)/shard_map/all_to_all | solution.py:103
  240.2 4.0 %fusion.104 = bf16[4096,1,128]{0,2,1:T(8,128)(2,1)} fusion(bf16[4096,1,128]{0,2,1:T(8,128)(2,1)} %fusion.134, bf16[1536,128]{1,0:T(8,128)(2,1)S(1)} %bitcast.237, f32[512,1536]{1,0:T(8,128)} %copy-done.5, f32[512]{0:T(512)S(1)} %get-tuple-element.33, f32[512]{0:T(512)S(1)} %fusion.26), kind=kOutput, calls=%fused_computation.90 | convolution fusion | flops 203030528 | bytes 3674112 | tf_op jit(solution)/shard_map/hqk,khe->qhe/dot_general | solution.py:50
  251.8 2.4 fusion.98
  254.7 2.7 reduce.32
  259.4 6.6 %all-to-all-start.6 = ((bf16[32,2,8192]{2,1,0:T(2,128)(2,1)}), bf16[32,2,8192]{2,1,0:T(2,128)(2,1)S(1)}, u32[]{:S(2)}, u32[]{:S(2)}) async-start(bf16[32,2,8192]{2,1,0:T(2,128)(2,1)} %reshape.506), calls=%async_computation.6 | async-start | bytes 2097152 | tf_op jit(solution)/shard_map/all_to_all | solution.py:109
  266.1 24.6 %all-to-all-done.6 = bf16[32,2,8192]{2,1,0:T(2,128)(2,1)S(1)} async-done(((bf16[32,2,8192]{2,1,0:T(2,128)(2,1)}), bf16[32,2,8192]{2,1,0:T(2,128)(2,1)S(1)}, u32[]{:S(2)}, u32[]{:S(2)}) %all-to-all-start.6) | async-done | bytes 1048608 | tf_op jit(solution)/shard_map/all_to_all | solution.py:109
  296.2 3.4 all_to_all.97
  299.6 8.9 %all-to-all-start.7 = ((bf16[16,12,4096]{2,1,0:T(8,128)(2,1)}), bf16[16,12,4096]{2,1,0:T(8,128)(2,1)}, u32[]{:S(2)}, u32[]{:S(2)}) async-start(bf16[16,12,4096]{2,1,0:T(8,128)(2,1)} %all_to_all.97), calls=%async_computation.7 | async-start | bytes 4194304 | tf_op jit(solution)/shard_map/all_to_all | solution.py:111
  308.6 49.0 %all-to-all-done.7 = bf16[16,12,4096]{2,1,0:T(8,128)(2,1)} async-done(((bf16[16,12,4096]{2,1,0:T(8,128)(2,1)}), bf16[16,12,4096]{2,1,0:T(8,128)(2,1)}, u32[]{:S(2)}, u32[]{:S(2)}) %all-to-all-start.7) | async-done | bytes 1572896 | tf_op jit(solution)/shard_map/all_to_all | solution.py:111
  357.6 2.5 all_to_all.99
  (188 shorter events, 78.1 us)
Async XLA Ops:
  5.6 33.1 %copy-start.39 = (s32[1,1,128]{2,1,0:T(1,128)S(1)}, s32[1,1,128]{2,1,0:T(1,128)}, u32[]{:S(2)}) copy-start(s32[1,1,128]{2,1,0:T(1,128)} %param.21) | copy-start | bytes 1540
  7.7 27.6 %all-to-all-start.4 = ((bf16[16,12,1024]{2,1,0:T(8,128)(2,1)}), bf16[16,12,1024]{2,1,0:T(8,128)(2,1)S(1)}, u32[]{:S(2)}, u32[]{:S(2)}) async-start(bf16[16,12,1024]{2,1,0:T(8,128)(2,1)} %all_to_all.88), calls=%async_computation.4 | async-start | bytes 1048576 | tf_op jit(solution)/shard_map/all_to_all | solution.py:80
  35.2 20.2 %all-to-all-start = ((bf16[16,12,1024]{2,1,0:T(8,128)(2,1)}), bf16[16,12,1024]{2,1,0:T(8,128)(2,1)S(1)}, u32[]{:S(2)}, u32[]{:S(2)}) async-start(bf16[16,12,1024]{2,1,0:T(8,128)(2,1)} %all_to_all.76), calls=%async_computation | async-start | bytes 1048576 | tf_op jit(solution)/shard_map/all_to_all | solution.py:83
  39.7 30.0 %copy-start.13 = (bf16[128,4096]{1,0:T(8,128)(2,1)S(1)}, bf16[128,4096]{1,0:T(8,128)(2,1)}, u32[]{:S(2)}) copy-start(bf16[128,4096]{1,0:T(8,128)(2,1)} %param.16) | copy-start | bytes 3145732
  58.5 39.2 %all-to-all-start.5 = ((bf16[128,32,128]{2,0,1:T(8,128)(2,1)}), bf16[128,32,128]{2,0,1:T(8,128)(2,1)S(1)}, u32[]{:S(2)}, u32[]{:S(2)}) async-start(bf16[128,32,128]{2,0,1:T(8,128)(2,1)} %bitcast.13), calls=%async_computation.5 | async-start | bytes 2097152 | tf_op jit(solution)/shard_map/all_to_all | solution.py:104
  97.7 54.3 %copy-start = (bf16[128,32,128]{2,0,1:T(8,128)(2,1)}, bf16[128,32,128]{2,0,1:T(8,128)(2,1)S(1)}, u32[]{:S(2)}) copy-start(bf16[128,32,128]{2,0,1:T(8,128)(2,1)S(1)} %all-to-all-done.5) | copy-start | bytes 3145732
  97.7 52.9 %all-to-all-start.2 = ((bf16[16,12,4096]{2,1,0:T(8,128)(2,1)}), bf16[16,12,4096]{2,1,0:T(8,128)(2,1)S(1)}, u32[]{:S(2)}, u32[]{:S(2)}) async-start(bf16[16,12,4096]{2,1,0:T(8,128)(2,1)} %all_to_all.82), calls=%async_computation.2 | async-start | bytes 4194304 | tf_op jit(solution)/shard_map/all_to_all | solution.py:77
  152.2 31.3 %all-to-all-start.1 = ((bf16[128,32,128]{2,0,1:T(8,128)(2,1)}), bf16[128,32,128]{2,0,1:T(8,128)(2,1)S(1)}, u32[]{:S(2)}, u32[]{:S(2)}) async-start(bf16[128,32,128]{2,0,1:T(8,128)(2,1)} %bitcast.229), calls=%async_computation.1 | async-start | bytes 2097152 | tf_op jit(solution)/shard_map/all_to_all | solution.py:105
  161.9 28.4 %copy-start.40 = (s32[1,1,8]{2,1,0:T(1,128)S(1)}, s32[1,1,8]{2,1,0:T(1,128)}, u32[]{:S(2)}) copy-start(s32[1,1,8]{2,1,0:T(1,128)} %param.19) | copy-start | bytes 100
  161.9 32.9 %copy-start.1 = (bf16[128,32,128]{2,0,1:T(8,128)(2,1)S(1)}, bf16[128,32,128]{2,0,1:T(8,128)(2,1)}, u32[]{:S(2)}) copy-start(bf16[128,32,128]{2,0,1:T(8,128)(2,1)} %copy-done) | copy-start | bytes 3145732
  183.5 32.2 %all-to-all-start.3 = ((bf16[128,32,128]{2,0,1:T(8,128)(2,1)}), bf16[128,32,128]{2,0,1:T(8,128)(2,1)S(1)}, u32[]{:S(2)}, u32[]{:S(2)}) async-start(bf16[128,32,128]{2,0,1:T(8,128)(2,1)} %copy_bitcast_fusion.1), calls=%async_computation.3 | async-start | bytes 2097152 | tf_op jit(solution)/shard_map/all_to_all | solution.py:103
  190.6 12.2 %copy-start.19 = (s32[4096]{0:T(1024)}, s32[4096]{0:T(1024)S(1)}, u32[]{:S(2)}) copy-start(s32[4096]{0:T(1024)S(1)} %convert_reduce_fusion) | copy-start | bytes 49156
  204.8 13.6 %slice-start.2 = ((s32[4096]{0:T(1024)}), s32[1024]{0:T(1024)S(1)}, s32[]{:S(2)}) async-start(s32[4096]{0:T(1024)} %copy-done.19), calls=%async_computation.10 | async-start | bytes 8192 | tf_op jit(solution)/shard_map/slice | solution.py:42
  204.8 13.6 %copy-start.31 = (s32[512]{0:T(512)S(1)}, s32[512]{0:T(512)}, u32[]{:S(2)}) copy-start(s32[512]{0:T(512)} %get-tuple-element.23) | copy-start | bytes 6148
  204.8 13.6 %copy-start.37 = (s32[512]{0:T(512)S(1)}, s32[512]{0:T(512)}, u32[]{:S(2)}) copy-start(s32[512]{0:T(512)} %iota_add_fusion.6) | copy-start | bytes 6148
  238.7 5.5 %copy-start.4 = (f32[512,2048]{1,0:T(8,128)S(1)}, f32[512,2048]{1,0:T(8,128)}, u32[]{:S(2)}) copy-start(f32[512,2048]{1,0:T(8,128)} %copy-done.3) | copy-start | bytes 12582916
  238.7 5.5 %copy-start.12 = (bf16[16,128,1,128]{3,1,0,2:T(8,128)(2,1)S(1)}, bf16[16,128,1,128]{3,1,0,2:T(8,128)(2,1)}, u32[]{:S(2)}) copy-start(bf16[16,128,1,128]{3,1,0,2:T(8,128)(2,1)} %slice.197) | copy-start | bytes 1572868
  239.0 6.8 %slice-start = ((s8[5242880]{0:T(1024)(128)(4,1)}), s8[4194304]{0:T(1024)(128)(4,1)S(1)}, s32[]{:S(2)}) async-start(s8[5242880]{0:T(1024)(128)(4,1)} %bitcast.226), calls=%async_computation.8 | async-start | bytes 8388608
  240.2 5.6 %slice-start.1 = ((s8[5242880]{0:T(1024)(128)(4,1)}), s8[1048576]{0:T(1024)(128)(4,1)S(1)}, s32[]{:S(2)}) async-start(s8[5242880]{0:T(1024)(128)(4,1)} %bitcast.226), calls=%async_computation.9 | async-start | bytes 2097152
  240.2 5.6 %copy-start.9 = (bf16[20,128,1,128]{3,1,0,2:T(8,128)(2,1)S(1)}, bf16[20,128,1,128]{3,1,0,2:T(8,128)(2,1)}, u32[]{:S(2)}) copy-start(bf16[20,128,1,128]{3,1,0,2:T(8,128)(2,1)} %slice.202) | copy-start | bytes 1966084
  254.7 11.4 %copy-start.38 = (s32[1,1,192]{2,1,0:T(1,128)S(1)}, s32[1,1,192]{2,1,0:T(1,128)}, u32[]{:S(2)}) copy-start(s32[1,1,192]{2,1,0:T(1,128)} %param.22) | copy-start | bytes 2308
  259.4 31.3 %all-to-all-start.6 = ((bf16[32,2,8192]{2,1,0:T(2,128)(2,1)}), bf16[32,2,8192]{2,1,0:T(2,128)(2,1)S(1)}, u32[]{:S(2)}, u32[]{:S(2)}) async-start(bf16[32,2,8192]{2,1,0:T(2,128)(2,1)} %reshape.506), calls=%async_computation.6 | async-start | bytes 2097152 | tf_op jit(solution)/shard_map/all_to_all | solution.py:109
  296.2 12.3 %copy-start.41 = (s32[1,1,128]{2,1,0:T(1,128)S(1)}, s32[1,1,128]{2,1,0:T(1,128)}, u32[]{:S(2)}) copy-start(s32[1,1,128]{2,1,0:T(1,128)} %param.23) | copy-start | bytes 1540
  299.6 58.0 %all-to-all-start.7 = ((bf16[16,12,4096]{2,1,0:T(8,128)(2,1)}), bf16[16,12,4096]{2,1,0:T(8,128)(2,1)}, u32[]{:S(2)}, u32[]{:S(2)}) async-start(bf16[16,12,4096]{2,1,0:T(8,128)(2,1)} %all_to_all.97), calls=%async_computation.7 | async-start | bytes 4194304 | tf_op jit(solution)/shard_map/all_to_all | solution.py:111
  (33 other events, 68.0 us)
where the time goes:
time: 370 us; the launch traced here: 363 us
  waiting for transfers between devices  205 us (55%)
  starting transfers between devices  56.2 us (15%)
  local copies, waits for them, and re-layouts  48.8 us (13%)
  matrix products  28.2 us (8%)
  other arithmetic  23.7 us (6%)
    all_to_all x1, waiting for transfers between devices, local(): lax.all_to_all(fill_slots(flat_out, back_pack[0, 0]), 'dp', split_axis=0,...  49 us
    all_to_all x1, waiting for transfers between devices, local(): lax.all_to_all(fill_slots(query_rows, send_table), 'dp', split_axis=0, co...  48 us
    all_to_all x1, waiting for transfers between devices, local(): lax.all_to_all(pack_outputs, 'ctx', split_axis=0, concat_axis=1, tiled=True)  24.6 us
    all_to_all x1, waiting for transfers between devices, local(): lax.all_to_all(local_k, 'ctx', split_axis=1, concat_axis=0, tiled=True)  22 us
    all_to_all x1, waiting for transfers between devices, local(): lax.all_to_all(local_v, 'ctx', split_axis=1, concat_axis=0, tiled=True)  19 us
    all_to_all x1, waiting for transfers between devices, local(): lax.all_to_all(fill_slots(rotated_key_rows, send_table), 'dp', split_axis...  16.4 us
    dot_general x8, matrix products, attend(): jnp.einsum('hqk,khe->qhe', probabilities, value_per_head[:end_row], prefe...  16.1 us
    all_to_all x1, waiting for transfers between devices, local(): lax.all_to_all(fill_slots(value_head_rows, send_table), 'dp', split_axis=...  15.7 us
  transfers between devices with their start and end apart: 8, of which 8 were waited for; matrix products, arithmetic and copies ran while one was open for 7% of the time, Pallas kernels for 0%

commit v1 on v0

v1 whole, which is shorter than its diff:
```python
import math

import jax
import jax.numpy as jnp
from jax import lax
from jax.experimental import pallas as pl
from jax.experimental.pallas import tpu as pltpu
from jax.sharding import Mesh, PartitionSpec as P

QUERY_HEADS = 32
KEY_VALUE_HEADS = 8
HEAD_SIZE = 128
GROUP_HEADS = QUERY_HEADS // KEY_VALUE_HEADS
CAP = 12
N_DP = 16
N_Z = 8
N_X = 4
SLAB = 128
DOCS = 8
MOST = 2048
Q_ROWS = GROUP_HEADS * CAP
KV_ROWS = 2 * CAP
PAIR = 2 * SLAB
MAX_PAIRS = MOST // PAIR + 1
EXP2_SCALE = math.log2(math.e) / math.sqrt(HEAD_SIZE)
MASKED = -1e30
VMEM_BYTES = 40 * 1024 * 1024
EXCHANGE = ("y", "core", "z")


def slot_rows(code, heads):
    peer = (code * 171) >> 11
    base = peer * (heads * CAP) + (code - peer * CAP)
    return jnp.concatenate([base + h * CAP for h in range(heads)], axis=1)


def one_hot(rows, targets):
    at = lax.broadcasted_iota(jnp.int32, (rows, targets.shape[1]), 0)
    return jnp.where(at == targets, 1.0, 0.0).astype(jnp.bfloat16)


def contract(a, b, dim_a, dim_b):
    return lax.dot_general(
        a, b, (((dim_a,), (dim_b,)), ((), ())), preferred_element_type=jnp.float32
    )


def pack_kv_kernel(code_ref, key_ref, value_ref, out_ref):
    select = one_hot(N_DP * KV_ROWS, slot_rows(code_ref[...], 2))
    rows = jnp.concatenate([key_ref[...], value_ref[...]], axis=0)
    sent = contract(select, rows, 1, 0).astype(jnp.bfloat16)
    for z in range(N_Z):
        piece = sent[:, z * HEAD_SIZE : (z + 1) * HEAD_SIZE]
        out_ref[:, z] = piece.reshape(N_DP, KV_ROWS, HEAD_SIZE)


def pack_q_kernel(code_ref, query_ref, out_ref):
    select = one_hot(N_DP * Q_ROWS, slot_rows(code_ref[...], GROUP_HEADS))
    for z in range(N_Z):
        first = z * GROUP_HEADS
        rows = jnp.concatenate(
            [
                query_ref[:, (first + h) * HEAD_SIZE : (first + h + 1) * HEAD_SIZE]
                for h in range(GROUP_HEADS)
            ],
            axis=0,
        )
        sent = contract(select, rows, 1, 0).astype(jnp.bfloat16)
        out_ref[:, z] = sent.reshape(N_DP, Q_ROWS, HEAD_SIZE)


def place_kv_kernel(code_ref, slots_ref, out_ref):
    for z in range(N_Z):
        select = one_hot(N_DP * KV_ROWS, slot_rows(code_ref[z : z + 1, :], 2))
        slots = slots_ref[:, z].reshape(N_DP * KV_ROWS, HEAD_SIZE)
        keys = contract(select[:, :SLAB], slots, 0, 0)
        values_t = contract(slots, select[:, SLAB:], 0, 0)
        out_ref[z, :SLAB] = keys.astype(jnp.bfloat16)
        out_ref[z, SLAB:] = values_t.astype(jnp.bfloat16)


def attend_kernel(lengths_ref, lane_ref, code_ref, slots_ref, kv_ref, out_ref, scores_ref, acc_ref):
    lane = lane_ref[0]
    bounds = []
    total = jnp.int32(0)
    for i in range(DOCS):
        total = total + lengths_ref[i]
        bounds.append(total)
    columns = GROUP_HEADS * SLAB
    in_slab = lax.broadcasted_iota(jnp.int32, (1, columns), 1) & (SLAB - 1)

    def slab(z, carry):
        first = (z * N_X + lane) * SLAB
        query_at = first + in_slab
        start = jnp.zeros((1, columns), jnp.int32)
        first_start = jnp.int32(0)
        for bound in bounds:
            start = jnp.where(query_at >= bound, bound, start)
            first_start = jnp.where(first >= bound, bound, first_start)
        pair_low = first_start // PAIR
        pairs = first // PAIR - pair_low + 1

        select = one_hot(N_DP * Q_ROWS, slot_rows(code_ref[pl.ds(z, 1), :], GROUP_HEADS))
        slots = slots_ref[:, z].reshape(N_DP * Q_ROWS, HEAD_SIZE)
        query_t = contract(slots, select, 0, 0).astype(jnp.bfloat16)

        def score(i, largest):
            pair = pair_low + i
            zk, xk = pair // 2, 2 * (pair % 2)
            keys = jnp.concatenate([kv_ref[xk, zk, :SLAB], kv_ref[xk + 1, zk, :SLAB]], axis=0)
            s = contract(keys, query_t, 1, 0)
            key_at = pair * PAIR + lax.broadcasted_iota(jnp.int32, (PAIR, columns), 0)
            s = jnp.where((key_at >= start) & (key_at <= query_at), s, MASKED)
            scores_ref[i] = s
            return jnp.maximum(largest, jnp.max(s.reshape(PAIR // 8, 8, columns), axis=0))

        largest = lax.fori_loop(0, pairs, score, jnp.full((8, columns), MASKED, jnp.float32))
        shift = jnp.max(largest, axis=0, keepdims=True) * EXP2_SCALE
        acc_ref[...] = jnp.zeros_like(acc_ref)

        def weigh(i, totals):
            pair = pair_low + i
            zk, xk = pair // 2, 2 * (pair % 2)
            weights = jnp.exp2(scores_ref[i] * EXP2_SCALE - shift)
            values_t = jnp.concatenate(
                [kv_ref[xk, zk, SLAB:], kv_ref[xk + 1, zk, SLAB:]], axis=1
            )
            acc_ref[...] += contract(values_t, weights.astype(jnp.bfloat16), 1, 0)
            return totals + jnp.sum(weights.reshape(PAIR // 8, 8, columns), axis=0)

        totals = lax.fori_loop(0, pairs, weigh, jnp.zeros((8, columns), jnp.float32))
        totals = jnp.sum(totals, axis=0, keepdims=True)
        attended_t = (acc_ref[...] / totals).astype(jnp.bfloat16)
        back = contract(select, attended_t, 1, 1).astype(jnp.bfloat16)
        out_ref[:, z] = back.reshape(N_DP, Q_ROWS, HEAD_SIZE)
        return carry

    lax.fori_loop(0, N_Z, slab, 0)


def unpack_kernel(code_ref, slots_ref, out_ref):
    select = one_hot(N_DP * Q_ROWS, slot_rows(code_ref[...], GROUP_HEADS))
    for z in range(N_Z):
        slots = slots_ref[:, z].reshape(N_DP * Q_ROWS, HEAD_SIZE)
        rows = contract(select, slots, 0, 0).astype(jnp.bfloat16)
        for h in range(GROUP_HEADS):
            at = (z * GROUP_HEADS + h) * HEAD_SIZE
            out_ref[:, at : at + HEAD_SIZE] = rows[h * SLAB : (h + 1) * SLAB]


def call(kernel, name, out_shape, specs, flops, moved, exps=0, scratch=()):
    return pl.pallas_call(
        kernel,
        name=name,
        out_shape=jax.ShapeDtypeStruct(out_shape, jnp.bfloat16),
        in_specs=[pl.BlockSpec(memory_space=s) for s in specs],
        out_specs=pl.BlockSpec(memory_space=pltpu.VMEM),
        scratch_shapes=scratch,
        compiler_params=pltpu.CompilerParams(vmem_limit_bytes=VMEM_BYTES),
        cost_estimate=pl.CostEstimate(flops=flops, bytes_accessed=moved, transcendentals=exps),
    )


def exchange(blocks):
    flat = blocks.reshape((N_DP * N_Z,) + blocks.shape[2:])
    flat = lax.all_to_all(flat, EXCHANGE, split_axis=0, concat_axis=0, tiled=True)
    return flat.reshape(blocks.shape)


def local(query, key, value, doc_lengths, send_slots, slab_source, back_pack, back_index):
    V, S = pltpu.VMEM, pltpu.SMEM
    columns = GROUP_HEADS * SLAB
    own_code = back_index.reshape(1, SLAB)
    q_blocks = (N_DP, N_Z, Q_ROWS, HEAD_SIZE)
    kv_blocks = (N_DP, N_Z, KV_ROWS, HEAD_SIZE)
    kv_sent = call(pack_kv_kernel, "pack_kv", kv_blocks, [V, V, V], 2 * 10**8, 2 * 10**6)(
        own_code, key, value
    )
    placed_code = lax.all_gather(slab_source.reshape(1, SLAB), "z", axis=0, tiled=True)
    kv_slots = exchange(kv_sent)
    q_sent = call(pack_q_kernel, "pack_q", q_blocks, [V, V], 8 * 10**8, 3 * 10**6)(
        own_code, query
    )
    q_sent, kv_slots = lax.optimization_barrier((q_sent, kv_slots))
    q_slots = exchange(q_sent)
    kv_placed = call(
        place_kv_kernel, "place_kv", (N_Z, 2 * SLAB, HEAD_SIZE), [V, V], 2 * 10**8, 2 * 10**6
    )(placed_code, kv_slots)
    kv_all = lax.all_gather(kv_placed, "x", axis=0, tiled=False)
    lane = lax.axis_index("x").astype(jnp.int32).reshape(1)
    out_sent = call(
        attend_kernel,
        "attend",
        q_blocks,
        [S, S, V, V, V],
        4 * 10**9,
        5 * 10**6,
        3 * 10**6,
        [
            pltpu.VMEM((MAX_PAIRS, PAIR, columns), jnp.float32),
            pltpu.VMEM((HEAD_SIZE, columns), jnp.float32),
        ],
    )(doc_lengths.reshape(DOCS), lane, placed_code, q_slots, kv_all)
    out_slots = exchange(out_sent)
    return call(
        unpack_kernel, "unpack", (SLAB, QUERY_HEADS * HEAD_SIZE), [V, V], 8 * 10**8, 3 * 10**6
    )(own_code, out_slots)


def solution(mesh):
    wide = Mesh(mesh.devices.reshape(N_DP // 2, 2, N_Z, N_X), ("y", "core", "z", "x"))
    rows = P(("y", "core", "z", "x"), None)
    table = P(("y", "core"), ("z", "x"), None)
    return jax.shard_map(
        local,
        mesh=wide,
        in_specs=(rows, rows, rows, P(("y", "core"), None, None), table, table, table, table),
        out_specs=rows,
        check_vma=False,
    )
```

time: 370 us -> 199 us (0.54); the launches traced: 363 us -> 199 us
  waiting for transfers between devices: 205 us -> 50.7 us
  blocking collectives: 0 us -> 66.4 us
  local copies, waits for them, and re-layouts: 48.8 us -> 4.19 us
  Pallas kernels: 0 us -> 28.3 us
  matrix products: 28.2 us -> 0 us
  other arithmetic: 23.7 us -> 0 us
  starting transfers between devices: 56.2 us -> 35.6 us
  between operations: 1.1 us -> 13.4 us
    all_to_all x8 -> x2, waiting for transfers between devices: 205 us -> 50.7 us  [exchange(): lax.all_to_all(flat, EXCHANGE, split_axis=0, concat_axis=0, tiled=True)]
    all_to_all x0 -> x1, blocking collectives: none -> 50.6 us  [exchange(): lax.all_to_all(flat, EXCHANGE, split_axis=0, concat_axis=0, tiled=True)]
    pallas_call x0 -> x5, Pallas kernels: none -> 28.3 us  [the longest x1 19.8 us: local(): call(attend_kernel, 'attend', q_blocks, [S, S, V, V, V], 4 * 10 ** 9, 5 *...]
    dot_general x16 -> x0, matrix products: 28.2 us -> none  [the longest x8 16.1 us: attend(): jnp.einsum('hqk,khe->qhe', probabilities, value_per_head[:end_row], prefe...]
    all_to_all x8 -> x2, starting transfers between devices: 56.2 us -> 35.6 us  [exchange(): lax.all_to_all(flat, EXCHANGE, split_axis=0, concat_axis=0, tiled=True)]
    all_gather x0 -> x1, blocking collectives: none -> 15.8 us  [local(): lax.all_gather(slab_source.reshape(1, SLAB), 'z', axis=0, tiled=True)]
    all_to_all x9 -> x0, local copies, waits for them, and re-layouts: 12.5 us -> none  [the longest x2 5.85 us: local(): lax.all_to_all(fill_slots(flat_out, back_pack[0, 0]), 'dp', split_axis=0,...]
    gather x8 -> x0, local copies, waits for them, and re-layouts: 11.5 us -> none  [the longest x4 6.39 us: fill_slots(): return jnp.take(padded, slot_table, axis=0)]
  transfers between devices with their start and end apart: 8 -> 3, of which waited for: 8 -> 2; matrix products, arithmetic and copies ran while one was open for 7% -> 0% of each run, Pallas kernels for 0% -> 1%
where the time goes in v1:
time: 199 us
  blocking collectives  66.4 us (33%)
  waiting for transfers between devices  50.7 us (25%)
  starting transfers between devices  35.6 us (18%)
  Pallas kernels  28.3 us (14%)
  between operations  13.4 us (7%)
  local copies, waits for them, and re-layouts  4.19 us (2%)
    all_to_all x2, waiting for transfers between devices, exchange(): lax.all_to_all(flat, EXCHANGE, split_axis=0, concat_axis=0, tiled=True)  50.7 us
    all_to_all x1, blocking collectives, exchange(): lax.all_to_all(flat, EXCHANGE, split_axis=0, concat_axis=0, tiled=True)  50.6 us
    all_to_all x2, starting transfers between devices, exchange(): lax.all_to_all(flat, EXCHANGE, split_axis=0, concat_axis=0, tiled=True)  35.6 us
    pallas_call x1, Pallas kernels, local(): call(attend_kernel, 'attend', q_blocks, [S, S, V, V, V], 4 * 10 ** 9, 5 *...  19.8 us
    all_gather x1, blocking collectives, local(): lax.all_gather(slab_source.reshape(1, SLAB), 'z', axis=0, tiled=True)  15.8 us
    unnamed x16, local copies, waits for them, and re-layouts  4.19 us
  transfers between devices with their start and end apart: 3, of which 2 were waited for; matrix products, arithmetic and copies ran while one was open for 0% of the time, Pallas kernels for 1%

profile of v1, /device:TPU:1, one launch (start us, length us, event | category | flops | bytes accessed | tf_op | source)
XLA Modules:
  0.0 198.7 jit_solution(11225783728207461150)
XLA Ops:
  6.5 0.0 copy-start.3
  6.5 0.0 copy-start.7
  6.5 1.0 copy-done
  7.5 0.9 copy-done.1
  8.5 0.7 copy-done.2
  9.1 1.3 pack_kv.1
  10.4 18.4 %all-to-all-start = ((bf16[128,24,128]{2,1,0:T(8,128)(2,1)}), bf16[128,24,128]{2,1,0:T(8,128)(2,1)S(1)}, u32[]{:S(2)}, u32[]{:S(2)}) async-start(bf16[128,24,128]{2,1,0:T(8,128)(2,1)} %bitcast.4), calls=%async_computation | async-start | bytes 1572864 | tf_op jit(solution)/shard_map/all_to_all | solution.py:166
  28.8 0.0 all-gather.4.cloned.1.call-start
  28.9 0.0 copy-done.7
  28.9 15.8 %all-gather = s32[8,1,128]{2,1,0:T(1,128)S(1)} all-gather(s32[1,1,128]{2,1,0:T(1,128)S(1)} %copy-done.7), channel_id=2, replica_groups=mesh['y'=8,'core'=2,'z'=8,'x'=4] {'z'}, dimensions={0}, use_global_device_ids=true | all-gather | bytes 4608 | tf_op jit(solution)/shard_map/all_gather | solution.py:179
  44.7 0.0 copy-done.3
  44.7 0.0 copy-done.5
  44.7 3.0 %pack_q.1 = bf16[16,8,48,128]{3,2,1,0:T(8,128)(2,1)} custom-call(s32[1,128]{1,0:T(1,128)S(1)} %bitcast.18, bf16[128,4096]{1,0:T(8,128)(2,1)S(1)} %copy-done.5), custom_call_target="tpu_custom_call" | custom-call | flops 800000000 | bytes 3000000 | tf_op jit(solution)/shard_map/pack_q/pallas_call | solution.py:181
  47.7 7.6 %all-to-all-done = bf16[128,24,128]{2,1,0:T(8,128)(2,1)S(1)} async-done(((bf16[128,24,128]{2,1,0:T(8,128)(2,1)}), bf16[128,24,128]{2,1,0:T(8,128)(2,1)S(1)}, u32[]{:S(2)}, u32[]{:S(2)}) %all-to-all-start) | async-done | bytes 786464 | tf_op jit(solution)/shard_map/all_to_all | solution.py:166
  55.3 1.4 place_kv.1
  56.7 0.0 all-gather.4.cloned.1.call-update
  56.8 0.0 copy-start.6
  56.8 17.1 %all-to-all-start.1 = ((bf16[128,48,128]{2,1,0:T(8,128)(2,1)}), bf16[128,48,128]{2,1,0:T(8,128)(2,1)S(1)}, u32[]{:S(2)}, u32[]{:S(2)}) async-start(bf16[128,48,128]{2,1,0:T(8,128)(2,1)} %bitcast.6), calls=%async_computation.1 | async-start | bytes 3145728 | tf_op jit(solution)/shard_map/all_to_all | solution.py:166
  73.9 43.1 %all-to-all-done.1 = bf16[128,48,128]{2,1,0:T(8,128)(2,1)S(1)} async-done(((bf16[128,48,128]{2,1,0:T(8,128)(2,1)}), bf16[128,48,128]{2,1,0:T(8,128)(2,1)S(1)}, u32[]{:S(2)}, u32[]{:S(2)}) %all-to-all-start.1) | async-done | bytes 1572896 | tf_op jit(solution)/shard_map/all_to_all | solution.py:166
  117.0 0.0 copy-done.6
  117.0 1.6 copy-done.4
  118.6 19.8 %attend.1 = bf16[16,8,48,128]{3,2,1,0:T(8,128)(2,1)S(1)} custom-call(s32[8]{0:T(128)S(1)} %bitcast.21, s32[1]{0:T(128)} %bitcast.2.lane_ref, s32[8,128]{1,0:T(8,128)S(1)} %bitcast.16, bf16[16,8,48,128]{3,2,1,0:T(8,128)(2,1)S(1)} %bitcast.12, bf16[4,8,256,128]{3,2,1,0:T(8,128)(2,1)S(1)} %bitcast.20), custom_call_target="tpu_custom_call" | custom-call | flops 4000000000 | bytes 5000000 | tf_op jit(solution)/shard_map/attend/pallas_call | solution.py:191
  138.5 50.6 %all_to_all.15 = bf16[128,48,128]{2,1,0:T(8,128)(2,1)S(1)} all-to-all(bf16[128,48,128]{2,1,0:T(8,128)(2,1)S(1)} %bitcast.13), channel_id=1, replica_groups=mesh['y'=8,'core'=2,'z'=8,'x'=4] {'y','core','z'}, dimensions={0} | all-to-all | bytes 3145728 | tf_op jit(solution)/shard_map/all_to_all | solution.py:166
  189.0 2.8 %unpack.1 = bf16[128,4096]{1,0:T(8,128)(2,1)} custom-call(s32[1,128]{1,0:T(1,128)S(1)} %bitcast.19, bf16[16,8,48,128]{3,2,1,0:T(8,128)(2,1)S(1)} %bitcast.14), custom_call_target="tpu_custom_call" | custom-call | flops 800000000 | bytes 3000000 | tf_op jit(solution)/shard_map/unpack/pallas_call | solution.py:205
  (6 shorter events, 0.0 us)
Async XLA Ops:
  6.5 38.2 %copy-start.3 = (s32[1,1,128]{2,1,0:T(1,128)S(1)}, s32[1,1,128]{2,1,0:T(1,128)}, u32[]{:S(2)}) copy-start(s32[1,1,128]{2,1,0:T(1,128)} %param.13) | copy-start | bytes 1540
  6.5 22.3 %copy-start.7 = (s32[1,1,128]{2,1,0:T(1,128)S(1)}, s32[1,1,128]{2,1,0:T(1,128)}, u32[]{:S(2)}) copy-start(s32[1,1,128]{2,1,0:T(1,128)} %param.12) | copy-start | bytes 1540
  6.5 1.0 copy-start
  7.5 0.9 copy-start.1
  8.5 0.7 copy-start.2
  9.1 35.6 %copy-start.5 = (bf16[128,4096]{1,0:T(8,128)(2,1)S(1)}, bf16[128,4096]{1,0:T(8,128)(2,1)}, u32[]{:S(2)}) copy-start(bf16[128,4096]{1,0:T(8,128)(2,1)} %query_ref.1) | copy-start | bytes 3145732
  10.4 44.9 %all-to-all-start = ((bf16[128,24,128]{2,1,0:T(8,128)(2,1)}), bf16[128,24,128]{2,1,0:T(8,128)(2,1)S(1)}, u32[]{:S(2)}, u32[]{:S(2)}) async-start(bf16[128,24,128]{2,1,0:T(8,128)(2,1)} %bitcast.4), calls=%async_computation | async-start | bytes 1572864 | tf_op jit(solution)/shard_map/all_to_all | solution.py:166
  28.8 88.2 %all-gather.4.cloned.1.call-start = ((), (), s32[]{:S(2)}) async-start(), calls=%async_computation.3 | async-start | bytes 2621440 | tf_op jit(solution)/shard_map/all_gather | solution.py:189
  56.8 60.3 %copy-start.6 = (s32[1,1,8]{2,1,0:T(1,128)S(1)}, s32[1,1,8]{2,1,0:T(1,128)}, u32[]{:S(2)}) copy-start(s32[1,1,8]{2,1,0:T(1,128)} %param.11) | copy-start | bytes 100
  56.8 60.2 %all-to-all-start.1 = ((bf16[128,48,128]{2,1,0:T(8,128)(2,1)}), bf16[128,48,128]{2,1,0:T(8,128)(2,1)S(1)}, u32[]{:S(2)}, u32[]{:S(2)}) async-start(bf16[128,48,128]{2,1,0:T(8,128)(2,1)} %bitcast.6), calls=%async_computation.1 | async-start | bytes 3145728 | tf_op jit(solution)/shard_map/all_to_all | solution.py:166
  117.0 1.6 copy-start.4
Sparse Core Ops, SparseCore 0:
  56.9 40.3 all-gather.3

commit v2 on v1

v2 whole, which is shorter than its diff:
```python
import math

import jax
import jax.numpy as jnp
from jax import lax
from jax.experimental import pallas as pl
from jax.experimental.pallas import tpu as pltpu
from jax.sharding import Mesh, PartitionSpec as P

QUERY_HEADS = 32
KEY_VALUE_HEADS = 8
HEAD_SIZE = 128
GROUP_HEADS = QUERY_HEADS // KEY_VALUE_HEADS
CAP = 12
N_DP = 16
N_Z = 8
N_X = 4
SLAB = 128
DOCS = 8
MOST = 2048
Q_ROWS = GROUP_HEADS * CAP
TABLE_AT = 2 * CAP
KV_ROWS = 32
PAIR = 2 * SLAB
MAX_PAIRS = MOST // PAIR + 1
STEPS = (4, 2, 1)
EXP2_SCALE = math.log2(math.e) / math.sqrt(HEAD_SIZE)
MASKED = -1e30
VMEM_BYTES = 24 * 1024 * 1024
EXCHANGE = ("y", "core", "z")


def slot_rows(code, heads, block_rows):
    peer = (code * 171) >> 11
    base = peer * block_rows + (code - peer * CAP)
    return jnp.concatenate([base + h * CAP for h in range(heads)], axis=1)


def one_hot(rows, targets):
    at = lax.broadcasted_iota(jnp.int32, (rows, targets.shape[1]), 0)
    return jnp.where(at == targets, 1.0, 0.0).astype(jnp.bfloat16)


def contract(a, b, dim_a, dim_b):
    return lax.dot_general(
        a, b, (((dim_a,), (dim_b,)), ((), ())), preferred_element_type=jnp.float32
    )


def pack_kv_kernel(
    code_ref, table_ref, key_ref, value_ref, out_ref, code, table, rows, sems
):
    copies = [
        pltpu.make_async_copy(code_ref, code, sems.at[0]),
        pltpu.make_async_copy(table_ref, table, sems.at[1]),
        pltpu.make_async_copy(key_ref, rows.at[:SLAB], sems.at[2]),
        pltpu.make_async_copy(value_ref, rows.at[SLAB:], sems.at[3]),
    ]
    for copy in copies:
        copy.start()
    for copy in copies:
        copy.wait()
    select = one_hot(N_DP * TABLE_AT, slot_rows(code[0], 2, TABLE_AT))
    sent = contract(select, rows[...], 1, 0).astype(jnp.bfloat16)
    codes = jnp.broadcast_to(
        table[0].astype(jnp.float32).astype(jnp.bfloat16)[None],
        (N_DP, KV_ROWS - TABLE_AT, SLAB),
    )
    for z in range(N_Z):
        piece = sent[:, z * HEAD_SIZE : (z + 1) * HEAD_SIZE]
        piece = piece.reshape(N_DP, TABLE_AT, HEAD_SIZE)
        out_ref[:, z] = jnp.concatenate([piece, codes], axis=1)


def pack_q_kernel(code_ref, query_ref, out_ref):
    select = one_hot(N_DP * Q_ROWS, slot_rows(code_ref[...], GROUP_HEADS, Q_ROWS))
    for z in range(N_Z):
        first = z * GROUP_HEADS
        rows = jnp.concatenate(
            [
                query_ref[:, (first + h) * HEAD_SIZE : (first + h + 1) * HEAD_SIZE]
                for h in range(GROUP_HEADS)
            ],
            axis=0,
        )
        sent = contract(select, rows, 1, 0).astype(jnp.bfloat16)
        out_ref[:, z] = sent.reshape(N_DP, Q_ROWS, HEAD_SIZE)


def place_kv_kernel(group_ref, slots_ref, out_ref, code_ref):
    group = group_ref[0]
    for z in range(N_Z):
        code = slots_ref[group, z, TABLE_AT:, :].astype(jnp.float32).astype(jnp.int32)[:1]
        code_ref[z : z + 1, :] = code
        select = one_hot(N_DP * KV_ROWS, slot_rows(code, 2, KV_ROWS))
        slots = slots_ref[:, z].reshape(N_DP * KV_ROWS, HEAD_SIZE)
        keys = contract(select[:, :SLAB], slots, 0, 0)
        values_t = contract(slots, select[:, SLAB:], 0, 0)
        out_ref[z, :SLAB] = keys.astype(jnp.bfloat16)
        out_ref[z, SLAB:] = values_t.astype(jnp.bfloat16)


def order_kv_kernel(gathered_ref, out_ref):
    for block in range(N_Z * N_X):
        z, x = block // N_X, block % N_X
        half = slice((block % 2) * SLAB, (block % 2 + 1) * SLAB)
        out_ref[block // 2, 0, half] = gathered_ref[x, z, :SLAB]
        out_ref[block // 2, 1, half] = gathered_ref[x, z, SLAB:]


def in_steps(count, sizes, body, carry):
    done = jnp.int32(0)
    for size in sizes:
        steps = (count - done) // size if size > 1 else count - done

        def step(i, carry, done=done, size=size):
            return body(done + i * size, size, carry)

        carry = lax.fori_loop(0, steps, step, carry)
        done = done + steps * size
    return carry


def attend_kernel(
    lengths_ref, lane_ref, code_ref, slots_ref, kv_ref, out_ref, scores_ref, acc_ref
):
    lane = lane_ref[0]
    bounds = []
    total = jnp.int32(0)
    for i in range(DOCS):
        total = total + lengths_ref[i]
        bounds.append(total)
    columns = GROUP_HEADS * SLAB
    in_slab = lax.broadcasted_iota(jnp.int32, (1, SLAB), 1)
    in_pair = lax.broadcasted_iota(jnp.int32, (PAIR, SLAB), 0)

    def slab(z, carry):
        first = (z * N_X + lane) * SLAB
        query_at = first + in_slab
        start = jnp.zeros((1, SLAB), jnp.int32)
        first_start = jnp.int32(0)
        for bound in bounds:
            start = jnp.where(query_at >= bound, bound, start)
            first_start = jnp.where(first >= bound, bound, first_start)
        pair_low = first_start // PAIR
        pairs = first // PAIR - pair_low + 1

        select = one_hot(
            N_DP * Q_ROWS, slot_rows(code_ref[pl.ds(z, 1), :], GROUP_HEADS, Q_ROWS)
        )
        slots = slots_ref[:, z].reshape(N_DP * Q_ROWS, HEAD_SIZE)
        query_t = contract(slots, select, 0, 0).astype(jnp.bfloat16)

        def score(i, size, largest):
            for r in range(size):
                at = (pair_low + i + r) * PAIR
                s = contract(kv_ref[pair_low + i + r, 0], query_t, 1, 0)
                allowed = (in_pair >= start - at) & (in_pair <= query_at - at)
                tops = []
                for h in range(GROUP_HEADS):
                    lanes = slice(h * SLAB, (h + 1) * SLAB)
                    masked = jnp.where(allowed, s[:, lanes], MASKED)
                    scores_ref[i + r, :, lanes] = masked
                    tops.append(jnp.max(masked.reshape(PAIR // 8, 8, SLAB), axis=0))
                largest = jnp.maximum(largest, jnp.concatenate(tops, axis=1))
            return largest

        largest = jnp.full((8, columns), MASKED, jnp.float32)
        largest = in_steps(pairs, STEPS, score, largest)
        shift = jnp.max(largest, axis=0, keepdims=True) * EXP2_SCALE
        acc_ref[...] = jnp.zeros_like(acc_ref)

        def weigh(i, size, totals):
            added = None
            for r in range(size):
                weights = jnp.exp2(scores_ref[i + r] * EXP2_SCALE - shift)
                values_t = jnp.concatenate(
                    [
                        kv_ref[pair_low + i + r, 1, :SLAB],
                        kv_ref[pair_low + i + r, 1, SLAB:],
                    ],
                    axis=1,
                )
                part = contract(values_t, weights.astype(jnp.bfloat16), 1, 0)
                added = part if added is None else added + part
                totals = totals + jnp.sum(weights.reshape(PAIR // 8, 8, columns), axis=0)
            acc_ref[...] += added
            return totals

        totals = in_steps(pairs, STEPS, weigh, jnp.zeros((8, columns), jnp.float32))
        totals = jnp.sum(totals, axis=0, keepdims=True)
        attended_t = (acc_ref[...] / totals).astype(jnp.bfloat16)
        back = contract(select, attended_t, 1, 1).astype(jnp.bfloat16)
        out_ref[:, z] = back.reshape(N_DP, Q_ROWS, HEAD_SIZE)
        return carry

    lax.fori_loop(0, N_Z, slab, 0)


def unpack_kernel(targets_ref, slots_ref, out_ref):
    select = one_hot(GROUP_HEADS * SLAB, targets_ref[...])
    for z in range(N_Z):
        slots = slots_ref[:, z].reshape(N_DP * Q_ROWS, HEAD_SIZE)
        rows = contract(select, slots, 1, 0).astype(jnp.bfloat16)
        for h in range(GROUP_HEADS):
            at = (z * GROUP_HEADS + h) * HEAD_SIZE
            out_ref[:, at : at + HEAD_SIZE] = rows[h * SLAB : (h + 1) * SLAB]


def call(kernel, name, outs, specs, flops, moved, exps=0, scratch=(), vmem=VMEM_BYTES):
    return pl.pallas_call(
        kernel,
        name=name,
        out_shape=[jax.ShapeDtypeStruct(shape, dtype) for shape, dtype in outs],
        in_specs=[pl.BlockSpec(memory_space=s) for s in specs],
        out_specs=[pl.BlockSpec(memory_space=pltpu.VMEM)] * len(outs),
        scratch_shapes=scratch,
        compiler_params=pltpu.CompilerParams(vmem_limit_bytes=vmem),
        cost_estimate=pl.CostEstimate(flops=flops, bytes_accessed=moved, transcendentals=exps),
    )


def exchange(blocks):
    flat = blocks.reshape((N_DP * N_Z,) + blocks.shape[2:])
    flat = lax.all_to_all(flat, EXCHANGE, split_axis=0, concat_axis=0, tiled=True)
    return flat.reshape(blocks.shape)


def local(query, key, value, doc_lengths, send_slots, slab_source, back_pack, back_index):
    V, S, H = pltpu.VMEM, pltpu.SMEM, pl.ANY
    half, whole = jnp.bfloat16, jnp.int32
    columns = GROUP_HEADS * SLAB
    q_blocks = (N_DP, N_Z, Q_ROWS, HEAD_SIZE)
    kv_blocks = (N_DP, N_Z, KV_ROWS, HEAD_SIZE)
    (kv_sent,) = call(
        pack_kv_kernel,
        "pack_kv",
        [(kv_blocks, half)],
        [H, H, H, H],
        2 * 10**8,
        2 * 10**6,
        0,
        [
            V((1, 1, SLAB), whole),
            V((1, 1, SLAB), whole),
            V((2 * SLAB, KEY_VALUE_HEADS * HEAD_SIZE), half),
            pltpu.SemaphoreType.DMA((4,)),
        ],
        60 * 1024 * 1024,
    )(back_index, slab_source, key, value)
    kv_slots = exchange(kv_sent)
    own_code = back_index.reshape(1, SLAB)
    (q_sent,) = call(pack_q_kernel, "pack_q", [(q_blocks, half)], [V, V], 8 * 10**8, 3 * 10**6)(
        own_code, query
    )
    q_sent, kv_slots = lax.optimization_barrier((q_sent, kv_slots))
    q_slots = exchange(q_sent)
    group = lax.axis_index(("y", "core")).astype(whole).reshape(1)
    kv_placed, code = call(
        place_kv_kernel,
        "place_kv",
        [((N_Z, 2 * SLAB, HEAD_SIZE), half), ((N_Z, SLAB), whole)],
        [S, V],
        2 * 10**8,
        2 * 10**6,
    )(group, kv_slots)
    kv_all = lax.all_gather(kv_placed, "x", axis=0, tiled=False)
    (kv_pairs,) = call(
        order_kv_kernel,
        "order_kv",
        [((N_Z * N_X // 2, 2, PAIR, HEAD_SIZE), half)],
        [V],
        10**6,
        4 * 10**6,
    )(kv_all)
    lane = lax.axis_index("x").astype(whole).reshape(1)
    (out_sent,) = call(
        attend_kernel,
        "attend",
        [(q_blocks, half)],
        [S, S, V, V, V],
        4 * 10**9,
        5 * 10**6,
        3 * 10**6,
        [V((MAX_PAIRS, PAIR, columns), jnp.float32), V((HEAD_SIZE, columns), jnp.float32)],
    )(doc_lengths.reshape(DOCS), lane, code, q_slots, kv_pairs)
    out_slots = exchange(out_sent)
    sent = send_slots.reshape(N_DP, 1, CAP)
    head = jnp.arange(GROUP_HEADS, dtype=whole).reshape(1, GROUP_HEADS, 1)
    targets = jnp.where(sent < SLAB, sent + head * SLAB, -1).reshape(1, N_DP * Q_ROWS)
    (out,) = call(
        unpack_kernel,
        "unpack",
        [((SLAB, QUERY_HEADS * HEAD_SIZE), half)],
        [V, V],
        8 * 10**8,
        3 * 10**6,
    )(targets, out_slots)
    return out


def solution(mesh):
    wide = Mesh(mesh.devices.reshape(N_DP // 2, 2, N_Z, N_X), ("y", "core", "z", "x"))
    rows = P(("y", "core", "z", "x"), None)
    table = P(("y", "core"), ("z", "x"), None)
    return jax.shard_map(
        local,
        mesh=wide,
        in_specs=(rows, rows, rows, P(("y", "core"), None, None), table, table, table, table),
        out_specs=rows,
        check_vma=False,
    )
```

time: 199 us -> 187 us (0.940)
  blocking collectives: 66.4 us -> 0 us
  waiting for transfers between devices: 50.7 us -> 111 us
  starting transfers between devices: 35.6 us -> 30.7 us
    all_to_all x1 -> x0, blocking collectives: 50.6 us -> none  [exchange(): lax.all_to_all(flat, EXCHANGE, split_axis=0, concat_axis=0, tiled=True)]
    all_to_all x2 -> x3, waiting for transfers between devices: 50.7 us -> 88.7 us  [exchange(): lax.all_to_all(flat, EXCHANGE, split_axis=0, concat_axis=0, tiled=True)]
    all_gather x1, waiting for transfers between devices: 0.01 us -> 22.1 us  [local(): kv_all = lax.all_gather(kv_placed, 'x', axis=0, tiled=False)]
    all_gather x1 -> x0, blocking collectives: 15.8 us -> none  [local(): lax.all_gather(slab_source.reshape(1, SLAB), 'z', axis=0, tiled=True)]
    all_to_all x2 -> x3, starting transfers between devices: 35.6 us -> 30.6 us  [exchange(): lax.all_to_all(flat, EXCHANGE, split_axis=0, concat_axis=0, tiled=True)]
    pallas_call x5 -> x6, Pallas kernels: 28.3 us -> 27.3 us  [the longest x1 17.3 us: local(): call(attend_kernel, 'attend', [(q_blocks, half)], [S, S, V, V, V], 4 * 10...]
    unnamed x16 -> x13, local copies, waits for them, and re-layouts: 4.19 us -> 3.27 us
  transfers between devices with their start and end apart: 3 -> 4, of which waited for: 2 -> 4; matrix products, arithmetic and copies ran while one was open for 0% -> 1% of each run, Pallas kernels for 1% -> 2%
where the time goes in v2:
time: 187 us
  waiting for transfers between devices  111 us (59%)
  starting transfers between devices  30.7 us (16%)
  Pallas kernels  27.3 us (15%)
  between operations  13.5 us (7%)
  local copies, waits for them, and re-layouts  3.47 us (2%)
    all_to_all x3, waiting for transfers between devices, exchange(): lax.all_to_all(flat, EXCHANGE, split_axis=0, concat_axis=0, tiled=True)  88.7 us
    all_to_all x3, starting transfers between devices, exchange(): lax.all_to_all(flat, EXCHANGE, split_axis=0, concat_axis=0, tiled=True)  30.6 us
    all_gather x1, waiting for transfers between devices, local(): kv_all = lax.all_gather(kv_placed, 'x', axis=0, tiled=False)  22.1 us
    pallas_call x1, Pallas kernels, local(): call(attend_kernel, 'attend', [(q_blocks, half)], [S, S, V, V, V], 4 * 10...  17.3 us
  transfers between devices with their start and end apart: 4, of which 4 were waited for; matrix products, arithmetic and copies ran while one was open for 1% of the time, Pallas kernels for 2%

profile of v2, /device:TPU:1, one launch (start us, length us, event | category | flops | bytes accessed | tf_op | source)
XLA Modules:
  0.0 186.6 jit_solution(10951464051806085673)
XLA Ops:
  6.5 2.5 %pack_kv.1 = bf16[16,8,32,128]{3,2,1,0:T(8,128)(2,1)} custom-call(s32[1,1,128]{2,1,0:T(1,128)} %code_ref.1, s32[1,1,128]{2,1,0:T(1,128)} %table_ref.1, bf16[128,1024]{1,0:T(8,128)(2,1)} %key_ref.1, bf16[128,1024]{1,0:T(8,128)(2,1)} %value_ref.1), custom_call_target="tpu_custom_call" | custom-call | flops 200000000 | bytes 2000000 | tf_op jit(solution)/shard_map/pack_kv/pallas_call | solution.py:235
  9.1 18.4 %all-to-all-start = ((bf16[128,32,128]{2,1,0:T(8,128)(2,1)}), bf16[128,32,128]{2,1,0:T(8,128)(2,1)S(1)}, u32[]{:S(2)}, u32[]{:S(2)}) async-start(bf16[128,32,128]{2,1,0:T(8,128)(2,1)} %bitcast.17), calls=%async_computation | async-start | bytes 2097152 | tf_op jit(solution)/shard_map/all_to_all | solution.py:225
  27.5 0.0 all-gather.3.cloned.1.call-start
  27.6 0.0 copy-done.2
  27.6 3.0 %pack_q.1 = bf16[16,8,48,128]{3,2,1,0:T(8,128)(2,1)} custom-call(s32[1,128]{1,0:T(1,128)S(1)} %bitcast.15, bf16[128,4096]{1,0:T(8,128)(2,1)S(1)} %copy-done.3), custom_call_target="tpu_custom_call" | custom-call | flops 800000000 | bytes 3000000 | tf_op jit(solution)/shard_map/pack_q/pallas_call | solution.py:253
  30.6 29.0 %all-to-all-done = bf16[128,32,128]{2,1,0:T(8,128)(2,1)S(1)} async-done(((bf16[128,32,128]{2,1,0:T(8,128)(2,1)}), bf16[128,32,128]{2,1,0:T(8,128)(2,1)S(1)}, u32[]{:S(2)}, u32[]{:S(2)}) %all-to-all-start) | async-done | bytes 1048608 | tf_op jit(solution)/shard_map/all_to_all | solution.py:225
  59.6 1.7 place_kv.1
  61.3 0.0 all-gather.3.cloned.1.call-update
  61.3 6.4 %all-to-all-start.1 = ((bf16[128,48,128]{2,1,0:T(8,128)(2,1)}), bf16[128,48,128]{2,1,0:T(8,128)(2,1)}, u32[]{:S(2)}, u32[]{:S(2)}) async-start(bf16[128,48,128]{2,1,0:T(8,128)(2,1)} %bitcast.6), calls=%async_computation.1 | async-start | bytes 3145728 | tf_op jit(solution)/shard_map/all_to_all | solution.py:225
  67.7 22.1 %all-gather.3.cloned.1.call-done = bf16[32,256,128]{2,1,0:T(8,128)(2,1)} async-done(((bf16[8,256,128]{2,1,0:T(8,128)(2,1)}), bf16[32,256,128]{2,1,0:T(8,128)(2,1)}) %all-gather.3.cloned.1.call-update) | async-done | bytes 2097168 | tf_op jit(solution)/shard_map/all_gather | solution.py:267
  89.8 1.6 copy-done
  91.4 0.1 order_kv.1.kv_ref
  91.5 18.1 %all-to-all-done.1 = bf16[128,48,128]{2,1,0:T(8,128)(2,1)} async-done(((bf16[128,48,128]{2,1,0:T(8,128)(2,1)}), bf16[128,48,128]{2,1,0:T(8,128)(2,1)}, u32[]{:S(2)}, u32[]{:S(2)}) %all-to-all-start.1) | async-done | bytes 1572896 | tf_op jit(solution)/shard_map/all_to_all | solution.py:225
  109.6 17.3 %attend.1 = bf16[16,8,48,128]{3,2,1,0:T(8,128)(2,1)S(1)} custom-call(s32[8]{0:T(128)S(1)} %bitcast.16, s32[1]{0:T(128)} %bitcast.1.lane_ref, s32[8,128]{1,0:T(8,128)S(1)} %get-tuple-element.10.code_ref, bf16[16,8,48,128]{3,2,1,0:T(8,128)(2,1)} %bitcast.7.slots_ref, bf16[16,2,256,128]{3,2,1,0:T(8,128)(2,1)S(1)} %order_kv.1.kv_ref), custom_call_target="tpu_custom_call" | custom-call | flops 4000000000 | bytes 5000000 | tf_op jit(solution)/shard_map/attend/pallas_call | solution.py:277
  126.9 1.2 copy-done.1
  128.1 5.8 %all-to-all-start.2 = ((bf16[128,48,128]{2,1,0:T(8,128)(2,1)}), bf16[128,48,128]{2,1,0:T(8,128)(2,1)S(1)}, u32[]{:S(2)}, u32[]{:S(2)}) async-start(bf16[128,48,128]{2,1,0:T(8,128)(2,1)} %bitcast.14), calls=%async_computation.2 | async-start | bytes 3145728 | tf_op jit(solution)/shard_map/all_to_all | solution.py:225
  133.9 0.5 broadcast.33
  134.4 0.0 copy-done.5
  134.4 0.7 reduce.3
  135.1 0.1 reshape.84
  135.2 0.1 add_select_fusion
  135.2 0.1 select_n.15.targets_ref
  135.4 41.6 %all-to-all-done.2 = bf16[128,48,128]{2,1,0:T(8,128)(2,1)S(1)} async-done(((bf16[128,48,128]{2,1,0:T(8,128)(2,1)}), bf16[128,48,128]{2,1,0:T(8,128)(2,1)S(1)}, u32[]{:S(2)}, u32[]{:S(2)}) %all-to-all-start.2) | async-done | bytes 1572896 | tf_op jit(solution)/shard_map/all_to_all | solution.py:225
  177.0 2.8 %unpack.1 = bf16[128,4096]{1,0:T(8,128)(2,1)} custom-call(s32[1,768]{1,0:T(1,128)S(1)} %select_n.15.targets_ref, bf16[16,8,48,128]{3,2,1,0:T(8,128)(2,1)S(1)} %bitcast.13), custom_call_target="tpu_custom_call" | custom-call | flops 800000000 | bytes 3000000 | tf_op jit(solution)/shard_map/unpack/pallas_call | solution.py:291
  (10 shorter events, 0.0 us)
Async XLA Ops:
  6.5 21.0 %copy-start.2 = (s32[1,1,128]{2,1,0:T(1,128)S(1)}, s32[1,1,128]{2,1,0:T(1,128)}, u32[]{:S(2)}) copy-start(s32[1,1,128]{2,1,0:T(1,128)} %code_ref.1) | copy-start | bytes 1540
  6.5 21.0 %copy-start.3 = (bf16[128,4096]{1,0:T(8,128)(2,1)S(1)}, bf16[128,4096]{1,0:T(8,128)(2,1)}, u32[]{:S(2)}) copy-start(bf16[128,4096]{1,0:T(8,128)(2,1)} %query_ref.1) | copy-start | bytes 3145732
  9.1 50.5 %all-to-all-start = ((bf16[128,32,128]{2,1,0:T(8,128)(2,1)}), bf16[128,32,128]{2,1,0:T(8,128)(2,1)S(1)}, u32[]{:S(2)}, u32[]{:S(2)}) async-start(bf16[128,32,128]{2,1,0:T(8,128)(2,1)} %bitcast.17), calls=%async_computation | async-start | bytes 2097152 | tf_op jit(solution)/shard_map/all_to_all | solution.py:225
  27.5 62.3 %all-gather.3.cloned.1.call-start = ((), (), s32[]{:S(2)}) async-start(), calls=%async_computation.3 | async-start | bytes 2621440 | tf_op jit(solution)/shard_map/all_gather | solution.py:267
  61.3 48.4 %all-to-all-start.1 = ((bf16[128,48,128]{2,1,0:T(8,128)(2,1)}), bf16[128,48,128]{2,1,0:T(8,128)(2,1)}, u32[]{:S(2)}, u32[]{:S(2)}) async-start(bf16[128,48,128]{2,1,0:T(8,128)(2,1)} %bitcast.6), calls=%async_computation.1 | async-start | bytes 3145728 | tf_op jit(solution)/shard_map/all_to_all | solution.py:225
  89.8 1.6 copy-start
  91.4 18.2 %copy-start.4 = (s32[1,1,8]{2,1,0:T(1,128)S(1)}, s32[1,1,8]{2,1,0:T(1,128)}, u32[]{:S(2)}) copy-start(s32[1,1,8]{2,1,0:T(1,128)} %param.11) | copy-start | bytes 100
  126.9 1.2 copy-start.1
  128.1 6.3 %copy-start.5 = (s32[1,1,192]{2,1,0:T(1,128)S(1)}, s32[1,1,192]{2,1,0:T(1,128)}, u32[]{:S(2)}) copy-start(s32[1,1,192]{2,1,0:T(1,128)} %param.12) | copy-start | bytes 2308
  128.1 48.9 %all-to-all-start.2 = ((bf16[128,48,128]{2,1,0:T(8,128)(2,1)}), bf16[128,48,128]{2,1,0:T(8,128)(2,1)S(1)}, u32[]{:S(2)}, u32[]{:S(2)}) async-start(bf16[128,48,128]{2,1,0:T(8,128)(2,1)} %bitcast.14), calls=%async_computation.2 | async-start | bytes 3145728 | tf_op jit(solution)/shard_map/all_to_all | solution.py:225
Sparse Core Ops, SparseCore 0:
  61.4 28.3 all-gather.2

commit v3 on v2

--- a/solution.py
+++ b/solution.py
@@ -100,12 +100,12 @@
         out_ref[z, SLAB:] = values_t.astype(jnp.bfloat16)
 
 
-def order_kv_kernel(gathered_ref, out_ref):
-    for block in range(N_Z * N_X):
-        z, x = block // N_X, block % N_X
-        half = slice((block % 2) * SLAB, (block % 2 + 1) * SLAB)
-        out_ref[block // 2, 0, half] = gathered_ref[x, z, :SLAB]
-        out_ref[block // 2, 1, half] = gathered_ref[x, z, SLAB:]
+def order_kv_kernel(lane_ref, *refs):
+    out_ref = refs[N_X]
+    for back, piece_ref in enumerate(refs[:N_X]):
+        x = (lane_ref[0] - back) & (N_X - 1)
+        for z in range(N_Z):
+            out_ref[z * N_X + x] = piece_ref[z]
 
 
 def in_steps(count, sizes, body, carry):
@@ -154,7 +154,9 @@
         def score(i, size, largest):
             for r in range(size):
                 at = (pair_low + i + r) * PAIR
-                s = contract(kv_ref[pair_low + i + r, 0], query_t, 1, 0)
+                block = 2 * (pair_low + i + r)
+                keys = jnp.concatenate([kv_ref[block, :SLAB], kv_ref[block + 1, :SLAB]], axis=0)
+                s = contract(keys, query_t, 1, 0)
                 allowed = (in_pair >= start - at) & (in_pair <= query_at - at)
                 tops = []
                 for h in range(GROUP_HEADS):
@@ -174,12 +176,9 @@
             added = None
             for r in range(size):
                 weights = jnp.exp2(scores_ref[i + r] * EXP2_SCALE - shift)
+                block = 2 * (pair_low + i + r)
                 values_t = jnp.concatenate(
-                    [
-                        kv_ref[pair_low + i + r, 1, :SLAB],
-                        kv_ref[pair_low + i + r, 1, SLAB:],
-                    ],
-                    axis=1,
+                    [kv_ref[block, SLAB:], kv_ref[block + 1, SLAB:]], axis=1
                 )
                 part = contract(values_t, weights.astype(jnp.bfloat16), 1, 0)
                 added = part if added is None else added + part
@@ -264,16 +263,19 @@
         2 * 10**8,
         2 * 10**6,
     )(group, kv_slots)
-    kv_all = lax.all_gather(kv_placed, "x", axis=0, tiled=False)
-    (kv_pairs,) = call(
+    lane = lax.axis_index("x").astype(whole).reshape(1)
+    pieces = [kv_placed] + [
+        lax.ppermute(kv_placed, "x", [(x, (x + back) % N_X) for x in range(N_X)])
+        for back in range(1, N_X)
+    ]
+    (kv_blocks_all,) = call(
         order_kv_kernel,
         "order_kv",
-        [((N_Z * N_X // 2, 2, PAIR, HEAD_SIZE), half)],
-        [V],
+        [((N_Z * N_X, 2 * SLAB, HEAD_SIZE), half)],
+        [S] + [V] * N_X,
         10**6,
         4 * 10**6,
-    )(kv_all)
-    lane = lax.axis_index("x").astype(whole).reshape(1)
+    )(lane, *pieces)
     (out_sent,) = call(
         attend_kernel,
         "attend",
@@ -283,7 +285,7 @@
         5 * 10**6,
         3 * 10**6,
         [V((MAX_PAIRS, PAIR, columns), jnp.float32), V((HEAD_SIZE, columns), jnp.float32)],
-    )(doc_lengths.reshape(DOCS), lane, code, q_slots, kv_pairs)
+    )(doc_lengths.reshape(DOCS), lane, code, q_slots, kv_blocks_all)
     out_slots = exchange(out_sent)
     sent = send_slots.reshape(N_DP, 1, CAP)
     head = jnp.arange(GROUP_HEADS, dtype=whole).reshape(1, GROUP_HEADS, 1)

time: 187 us -> 172 us (0.920)
  waiting for transfers between devices: 111 us -> 97.3 us
  between operations: 13.5 us -> 0.14 us
  starting transfers between devices: 30.7 us -> 41.7 us
  local copies, waits for them, and re-layouts: 3.47 us -> 5.56 us
    all_gather x1 -> x0, waiting for transfers between devices: 22.1 us -> none  [local(): kv_all = lax.all_gather(kv_placed, 'x', axis=0, tiled=False)]
    ppermute x0 -> x3, waiting for transfers between devices: none -> 18.7 us  [local(): lax.ppermute(kv_placed, 'x', [(x, (x + back) % N_X) for x in range(N_X)])]
    ppermute x0 -> x3, starting transfers between devices: none -> 10.6 us  [local(): lax.ppermute(kv_placed, 'x', [(x, (x + back) % N_X) for x in range(N_X)])]
    all_to_all x3, waiting for transfers between devices: 88.7 us -> 78.7 us  [exchange(): lax.all_to_all(flat, EXCHANGE, split_axis=0, concat_axis=0, tiled=True)]
    unnamed x13 -> x19, local copies, waits for them, and re-layouts: 3.27 us -> 5.37 us
  transfers between devices with their start and end apart: 4 -> 6, of which waited for: 4 -> 6; matrix products, arithmetic and copies ran while one was open for 1% -> 1% of each run, Pallas kernels for 2% -> 2%
where the time goes in v3:
time: 172 us
  waiting for transfers between devices  97.3 us (57%)
  starting transfers between devices  41.7 us (24%)
  Pallas kernels  26.3 us (15%)
  local copies, waits for them, and re-layouts  5.56 us (3%)
    all_to_all x3, waiting for transfers between devices, exchange(): lax.all_to_all(flat, EXCHANGE, split_axis=0, concat_axis=0, tiled=True)  78.7 us
    all_to_all x3, starting transfers between devices, exchange(): lax.all_to_all(flat, EXCHANGE, split_axis=0, concat_axis=0, tiled=True)  31.1 us
    ppermute x3, waiting for transfers between devices, local(): lax.ppermute(kv_placed, 'x', [(x, (x + back) % N_X) for x in range(N_X)])  18.7 us
    pallas_call x1, Pallas kernels, local(): call(attend_kernel, 'attend', [(q_blocks, half)], [S, S, V, V, V], 4 * 10...  17.1 us
    ppermute x3, starting transfers between devices, local(): lax.ppermute(kv_placed, 'x', [(x, (x + back) % N_X) for x in range(N_X)])  10.6 us
    unnamed x19, local copies, waits for them, and re-layouts  5.37 us
  transfers between devices with their start and end apart: 6, of which 6 were waited for; matrix products, arithmetic and copies ran while one was open for 1% of the time, Pallas kernels for 2%

profile of v3, /device:TPU:1, one launch (start us, length us, event | category | flops | bytes accessed | tf_op | source)
XLA Modules:
  0.0 171.8 jit_solution(13316845043392715419)
XLA Ops:
  0.0 2.5 %pack_kv.1 = bf16[16,8,32,128]{3,2,1,0:T(8,128)(2,1)} custom-call(s32[1,1,128]{2,1,0:T(1,128)} %code_ref.1, s32[1,1,128]{2,1,0:T(1,128)} %table_ref.1, bf16[128,1024]{1,0:T(8,128)(2,1)} %key_ref.1, bf16[128,1024]{1,0:T(8,128)(2,1)} %value_ref.1), custom_call_target="tpu_custom_call" | custom-call | flops 200000000 | bytes 2000000 | tf_op jit(solution)/shard_map/pack_kv/pallas_call | solution.py:234
  2.5 18.4 %all-to-all-start = ((bf16[128,32,128]{2,1,0:T(8,128)(2,1)}), bf16[128,32,128]{2,1,0:T(8,128)(2,1)S(1)}, u32[]{:S(2)}, u32[]{:S(2)}) async-start(bf16[128,32,128]{2,1,0:T(8,128)(2,1)} %bitcast.15), calls=%async_computation | async-start | bytes 2097152 | tf_op jit(solution)/shard_map/all_to_all | solution.py:224
  21.0 2.9 %pack_q.1 = bf16[16,8,48,128]{3,2,1,0:T(8,128)(2,1)} custom-call(s32[1,128]{1,0:T(1,128)S(1)} %bitcast.13, bf16[128,4096]{1,0:T(8,128)(2,1)S(1)} %copy-done.6), custom_call_target="tpu_custom_call" | custom-call | flops 800000000 | bytes 3000000 | tf_op jit(solution)/shard_map/pack_q/pallas_call | solution.py:252
  23.9 29.1 %all-to-all-done = bf16[128,32,128]{2,1,0:T(8,128)(2,1)S(1)} async-done(((bf16[128,32,128]{2,1,0:T(8,128)(2,1)}), bf16[128,32,128]{2,1,0:T(8,128)(2,1)S(1)}, u32[]{:S(2)}, u32[]{:S(2)}) %all-to-all-start) | async-done | bytes 1048608 | tf_op jit(solution)/shard_map/all_to_all | solution.py:224
  53.0 6.4 %all-to-all-start.1 = ((bf16[128,48,128]{2,1,0:T(8,128)(2,1)}), bf16[128,48,128]{2,1,0:T(8,128)(2,1)}, u32[]{:S(2)}, u32[]{:S(2)}) async-start(bf16[128,48,128]{2,1,0:T(8,128)(2,1)} %bitcast.6), calls=%async_computation.1 | async-start | bytes 3145728 | tf_op jit(solution)/shard_map/all_to_all | solution.py:224
  59.4 0.9 place_kv.1
  60.3 3.2 %collective-permute-start = (bf16[8,256,128]{2,1,0:T(8,128)(2,1)S(1)}, bf16[8,256,128]{2,1,0:T(8,128)(2,1)S(1)}, u32[]{:S(2)}, u32[]{:S(2)}) collective-permute-start(bf16[8,256,128]{2,1,0:T(8,128)(2,1)S(1)} %get-tuple-element.12.refs_0_), channel_id=1, source_target_pairs={{0,1},{1,2},{2,3},{3,0},{4,5},{5,6},{6,7},{7,4},{8,9},{9,10},{10,1... | collective-permute-start | bytes 1572872 | tf_op jit(solution)/shard_map/ppermute | solution.py:268
  63.5 4.4 %collective-permute-start.1 = (bf16[8,256,128]{2,1,0:T(8,128)(2,1)S(1)}, bf16[8,256,128]{2,1,0:T(8,128)(2,1)S(1)}, u32[]{:S(2)}, u32[]{:S(2)}) collective-permute-start(bf16[8,256,128]{2,1,0:T(8,128)(2,1)S(1)} %get-tuple-element.12.refs_0_), channel_id=1, source_target_pairs={{0,2},{1,3},{2,0},{3,1},{4,6},{5,7},{6,4},{7,5},{8,10},{9,11},{10,... | collective-permute-start | bytes 1572872 | tf_op jit(solution)/shard_map/ppermute | solution.py:268
  67.8 3.1 %collective-permute-start.2 = (bf16[8,256,128]{2,1,0:T(8,128)(2,1)S(1)}, bf16[8,256,128]{2,1,0:T(8,128)(2,1)S(1)}, u32[]{:S(2)}, u32[]{:S(2)}) collective-permute-start(bf16[8,256,128]{2,1,0:T(8,128)(2,1)S(1)} %get-tuple-element.12.refs_0_), channel_id=1, source_target_pairs={{0,3},{1,0},{2,1},{3,2},{4,7},{5,4},{6,5},{7,6},{8,11},{9,8},{10,9... | collective-permute-start | bytes 1572872 | tf_op jit(solution)/shard_map/ppermute | solution.py:268
  70.9 6.0 %collective-permute-done.refs_1_ = bf16[8,256,128]{2,1,0:T(8,128)(2,1)S(1)} collective-permute-done((bf16[8,256,128]{2,1,0:T(8,128)(2,1)S(1)}, bf16[8,256,128]{2,1,0:T(8,128)(2,1)S(1)}, u32[]{:S(2)}, u32[]{:S(2)}) %collective-permute-start) | collective-permute-done | bytes 524320 | tf_op jit(solution)/shard_map/ppermute | solution.py:268
  76.9 12.3 %collective-permute-done.1.refs_2_ = bf16[8,256,128]{2,1,0:T(8,128)(2,1)S(1)} collective-permute-done((bf16[8,256,128]{2,1,0:T(8,128)(2,1)S(1)}, bf16[8,256,128]{2,1,0:T(8,128)(2,1)S(1)}, u32[]{:S(2)}, u32[]{:S(2)}) %collective-permute-start.1) | collective-permute-done | bytes 524320 | tf_op jit(solution)/shard_map/ppermute | solution.py:268
  89.3 0.8 copy-done.1
  90.0 0.3 collective-permute-done.2.refs_3_
  90.4 0.8 copy-done.3
  91.2 1.0 copy-done.2
  92.2 1.0 copy-done.4
  93.4 8.0 %all-to-all-done.1 = bf16[128,48,128]{2,1,0:T(8,128)(2,1)} async-done(((bf16[128,48,128]{2,1,0:T(8,128)(2,1)}), bf16[128,48,128]{2,1,0:T(8,128)(2,1)}, u32[]{:S(2)}, u32[]{:S(2)}) %all-to-all-start.1) | async-done | bytes 1572896 | tf_op jit(solution)/shard_map/all_to_all | solution.py:224
  101.4 17.1 %attend.1 = bf16[16,8,48,128]{3,2,1,0:T(8,128)(2,1)S(1)} custom-call(s32[8]{0:T(128)S(1)} %bitcast.14, s32[1]{0:T(128)} %bitcast.1.lane_ref, s32[8,128]{1,0:T(8,128)S(1)} %get-tuple-element.10.code_ref, bf16[16,8,48,128]{3,2,1,0:T(8,128)(2,1)} %bitcast.7.slots_ref, bf16[32,256,128]{2,1,0:T(8,128)(2,1)S(1)} %order_kv.1.kv_ref), custom_call_target="tpu_custom_call" | custom-call | flops 4000000000 | bytes 5000000 | tf_op jit(solution)/shard_map/attend/pallas_call | solution.py:279
  118.5 1.2 copy-done
  119.7 6.3 %all-to-all-start.2 = ((bf16[128,48,128]{2,1,0:T(8,128)(2,1)}), bf16[128,48,128]{2,1,0:T(8,128)(2,1)S(1)}, u32[]{:S(2)}, u32[]{:S(2)}) async-start(bf16[128,48,128]{2,1,0:T(8,128)(2,1)} %bitcast.12), calls=%async_computation.2 | async-start | bytes 3145728 | tf_op jit(solution)/shard_map/all_to_all | solution.py:224
  126.0 0.5 broadcast.33
  126.5 0.7 reduce.3
  127.5 41.6 %all-to-all-done.2 = bf16[128,48,128]{2,1,0:T(8,128)(2,1)S(1)} async-done(((bf16[128,48,128]{2,1,0:T(8,128)(2,1)}), bf16[128,48,128]{2,1,0:T(8,128)(2,1)S(1)}, u32[]{:S(2)}, u32[]{:S(2)}) %all-to-all-start.2) | async-done | bytes 1572896 | tf_op jit(solution)/shard_map/all_to_all | solution.py:224
  169.1 2.8 %unpack.1 = bf16[128,4096]{1,0:T(8,128)(2,1)} custom-call(s32[1,768]{1,0:T(1,128)S(1)} %select_n.15.targets_ref, bf16[16,8,48,128]{3,2,1,0:T(8,128)(2,1)S(1)} %bitcast.11), custom_call_target="tpu_custom_call" | custom-call | flops 800000000 | bytes 3000000 | tf_op jit(solution)/shard_map/unpack/pallas_call | solution.py:293
  (19 shorter events, 0.4 us)
Async XLA Ops:
  0.0 21.0 %copy-start.5 = (s32[1,1,128]{2,1,0:T(1,128)S(1)}, s32[1,1,128]{2,1,0:T(1,128)}, u32[]{:S(2)}) copy-start(s32[1,1,128]{2,1,0:T(1,128)} %code_ref.1) | copy-start | bytes 1540
  0.0 21.0 %copy-start.6 = (bf16[128,4096]{1,0:T(8,128)(2,1)S(1)}, bf16[128,4096]{1,0:T(8,128)(2,1)}, u32[]{:S(2)}) copy-start(bf16[128,4096]{1,0:T(8,128)(2,1)} %query_ref.1) | copy-start | bytes 3145732
  2.5 50.5 %all-to-all-start = ((bf16[128,32,128]{2,1,0:T(8,128)(2,1)}), bf16[128,32,128]{2,1,0:T(8,128)(2,1)S(1)}, u32[]{:S(2)}, u32[]{:S(2)}) async-start(bf16[128,32,128]{2,1,0:T(8,128)(2,1)} %bitcast.15), calls=%async_computation | async-start | bytes 2097152 | tf_op jit(solution)/shard_map/all_to_all | solution.py:224
  53.0 48.4 %all-to-all-start.1 = ((bf16[128,48,128]{2,1,0:T(8,128)(2,1)}), bf16[128,48,128]{2,1,0:T(8,128)(2,1)}, u32[]{:S(2)}, u32[]{:S(2)}) async-start(bf16[128,48,128]{2,1,0:T(8,128)(2,1)} %bitcast.6), calls=%async_computation.1 | async-start | bytes 3145728 | tf_op jit(solution)/shard_map/all_to_all | solution.py:224
  60.3 16.6 %collective-permute-start = (bf16[8,256,128]{2,1,0:T(8,128)(2,1)S(1)}, bf16[8,256,128]{2,1,0:T(8,128)(2,1)S(1)}, u32[]{:S(2)}, u32[]{:S(2)}) collective-permute-start(bf16[8,256,128]{2,1,0:T(8,128)(2,1)S(1)} %get-tuple-element.12.refs_0_), channel_id=1, source_target_pairs={{0,1},{1,2},{2,3},{3,0},{4,5},{5,6},{6,7},{7,4},{8,9},{9,10},{10,1... | collective-permute-start | bytes 1572872 | tf_op jit(solution)/shard_map/ppermute | solution.py:268
  63.5 25.8 %collective-permute-start.1 = (bf16[8,256,128]{2,1,0:T(8,128)(2,1)S(1)}, bf16[8,256,128]{2,1,0:T(8,128)(2,1)S(1)}, u32[]{:S(2)}, u32[]{:S(2)}) collective-permute-start(bf16[8,256,128]{2,1,0:T(8,128)(2,1)S(1)} %get-tuple-element.12.refs_0_), channel_id=1, source_target_pairs={{0,2},{1,3},{2,0},{3,1},{4,6},{5,7},{6,4},{7,5},{8,10},{9,11},{10,... | collective-permute-start | bytes 1572872 | tf_op jit(solution)/shard_map/ppermute | solution.py:268
  67.8 22.5 %collective-permute-start.2 = (bf16[8,256,128]{2,1,0:T(8,128)(2,1)S(1)}, bf16[8,256,128]{2,1,0:T(8,128)(2,1)S(1)}, u32[]{:S(2)}, u32[]{:S(2)}) collective-permute-start(bf16[8,256,128]{2,1,0:T(8,128)(2,1)S(1)} %get-tuple-element.12.refs_0_), channel_id=1, source_target_pairs={{0,3},{1,0},{2,1},{3,2},{4,7},{5,4},{6,5},{7,6},{8,11},{9,8},{10,9... | collective-permute-start | bytes 1572872 | tf_op jit(solution)/shard_map/ppermute | solution.py:268
  89.3 0.8 copy-start.1
  90.4 0.8 copy-start.3
  91.2 1.0 copy-start.2
  92.2 1.0 copy-start.4
  93.3 8.1 %copy-start.7 = (s32[1,1,8]{2,1,0:T(1,128)S(1)}, s32[1,1,8]{2,1,0:T(1,128)}, u32[]{:S(2)}) copy-start(s32[1,1,8]{2,1,0:T(1,128)} %param.11) | copy-start | bytes 100
  118.5 1.2 copy-start
  119.7 6.8 %copy-start.8 = (s32[1,1,192]{2,1,0:T(1,128)S(1)}, s32[1,1,192]{2,1,0:T(1,128)}, u32[]{:S(2)}) copy-start(s32[1,1,192]{2,1,0:T(1,128)} %param.12) | copy-start | bytes 2308
  119.7 49.4 %all-to-all-start.2 = ((bf16[128,48,128]{2,1,0:T(8,128)(2,1)}), bf16[128,48,128]{2,1,0:T(8,128)(2,1)S(1)}, u32[]{:S(2)}, u32[]{:S(2)}) async-start(bf16[128,48,128]{2,1,0:T(8,128)(2,1)} %bitcast.12), calls=%async_computation.2 | async-start | bytes 3145728 | tf_op jit(solution)/shard_map/all_to_all | solution.py:224

commit v4 on v3

v4 whole, which is shorter than its diff:
```python
import math

import jax
import jax.numpy as jnp
from jax import lax
from jax.experimental import pallas as pl
from jax.experimental.pallas import tpu as pltpu
from jax.sharding import Mesh, PartitionSpec as P

QUERY_HEADS = 32
KEY_VALUE_HEADS = 8
HEAD_SIZE = 128
GROUP_HEADS = QUERY_HEADS // KEY_VALUE_HEADS
CAP = 12
N_DP = 16
N_Z = 8
N_X = 4
SLAB = 128
DOCS = 8
MOST = 2048
WIDE = 2 * HEAD_SIZE
HEAD_PAIRS = GROUP_HEADS // 2
Q_ROWS = HEAD_PAIRS * CAP
KV_ROWS = 16
PAIR = 2 * SLAB
PAIR_BITS = 8
MAX_ITEMS = 48
STEPS = (8, 2, 1)
EXP2_SCALE = math.log2(math.e) / math.sqrt(HEAD_SIZE)
MASKED = -1e30
VMEM_BYTES = 24 * 1024 * 1024
EXCHANGE = ("y", "core", "z")


def slot_rows(code, runs, block_rows):
    peer = (code * 171) >> 11
    base = peer * block_rows + (code - peer * CAP)
    return jnp.concatenate([base + run * CAP for run in range(runs)], axis=1)


def one_hot(rows, targets):
    at = lax.broadcasted_iota(jnp.int32, (rows, targets.shape[1]), 0)
    return jnp.where(at == targets, 1.0, 0.0).astype(jnp.bfloat16)


def contract(a, b, dim_a, dim_b):
    return lax.dot_general(
        a, b, (((dim_a,), (dim_b,)), ((), ())), preferred_element_type=jnp.float32
    )


def pack_kv_kernel(
    code_ref, table_ref, key_ref, value_ref, out_ref, code, table, rows, sems
):
    copies = [
        pltpu.make_async_copy(code_ref, code, sems.at[0]),
        pltpu.make_async_copy(table_ref, table, sems.at[1]),
        pltpu.make_async_copy(key_ref, rows.at[:SLAB], sems.at[2]),
        pltpu.make_async_copy(value_ref, rows.at[SLAB:], sems.at[3]),
    ]
    for copy in copies:
        copy.start()
    for copy in copies:
        copy.wait()
    select = one_hot(N_DP * KV_ROWS, slot_rows(code[0], 1, KV_ROWS))
    codes = table[0].astype(jnp.float32)
    at = lax.broadcasted_iota(jnp.int32, (N_DP * KV_ROWS, WIDE), 0) & (KV_ROWS - 1)
    codes = jnp.where(at >= CAP, jnp.concatenate([codes, codes], axis=1), 0.0)
    for z in range(N_Z):
        lanes = slice(z * HEAD_SIZE, (z + 1) * HEAD_SIZE)
        both = jnp.concatenate([rows[:SLAB, lanes], rows[SLAB:, lanes]], axis=1)
        sent = (contract(select, both, 1, 0) + codes).astype(jnp.bfloat16)
        out_ref[:, z] = sent.reshape(N_DP, KV_ROWS, WIDE)


def pack_q_kernel(code_ref, query_ref, out_ref):
    select = one_hot(N_DP * Q_ROWS, slot_rows(code_ref[...], HEAD_PAIRS, Q_ROWS))
    for z in range(N_Z):
        first = z * HEAD_PAIRS
        rows = jnp.concatenate(
            [query_ref[:, (first + p) * WIDE : (first + p + 1) * WIDE] for p in range(HEAD_PAIRS)],
            axis=0,
        )
        sent = contract(select, rows, 1, 0).astype(jnp.bfloat16)
        out_ref[:, z] = sent.reshape(N_DP, Q_ROWS, WIDE)


def place_kv_kernel(group_ref, slots_ref, out_ref, code_ref):
    group = group_ref[0]
    for z in range(N_Z):
        own = slots_ref[group, z].astype(jnp.float32).astype(jnp.int32)
        code = own[CAP : CAP + 1, :SLAB]
        code_ref[z : z + 1, :] = code
        select = one_hot(N_DP * KV_ROWS, slot_rows(code, 1, KV_ROWS))
        slots = slots_ref[:, z].reshape(N_DP * KV_ROWS, WIDE)
        keys = contract(select, slots[:, :HEAD_SIZE], 0, 0)
        values_t = contract(slots[:, HEAD_SIZE:], select, 0, 0)
        out_ref[z, :SLAB] = keys.astype(jnp.bfloat16)
        out_ref[z, SLAB:] = values_t.astype(jnp.bfloat16)


def order_kv_kernel(lane_ref, *refs):
    out_ref = refs[N_X]
    for back, piece_ref in enumerate(refs[:N_X]):
        x = (lane_ref[0] - back) & (N_X - 1)
        for z in range(N_Z):
            out_ref[z * N_X + x] = piece_ref[z]


def each_item(items, end_of, body):
    done, slab = jnp.int32(0), jnp.int32(0)
    for size in STEPS:
        steps = (items - done) // size if size > 1 else items - done

        def step(i, slab, done=done, size=size):
            for r in range(size):
                item = done + i * size + r
                slab = jnp.where(item >= end_of[slab], slab + 1, slab)
                body(item, slab)
            return slab

        slab = lax.fori_loop(0, steps, step, slab)
        done = done + steps * size


def attend_kernel(
    lengths_ref,
    lane_ref,
    code_ref,
    slots_hbm,
    kv_ref,
    out_hbm,
    slots_ref,
    out_ref,
    select_ref,
    query_ref,
    scores_ref,
    tops_ref,
    sums_ref,
    acc_ref,
    low_of,
    end_of,
    in_sems,
    out_sems,
):
    lane = lane_ref[0]
    columns = GROUP_HEADS * SLAB

    def copy_in(z):
        return pltpu.make_async_copy(slots_hbm.at[:, z], slots_ref.at[z], in_sems.at[z])

    def copy_out(z):
        return pltpu.make_async_copy(out_ref.at[z], out_hbm.at[:, z], out_sems.at[z])

    for z in range(N_Z):
        copy_in(z).start()

    bounds = []
    total = jnp.int32(0)
    for i in range(DOCS):
        total = total + lengths_ref[i]
        bounds.append(total)

    items = jnp.int32(0)
    for z in range(N_Z):
        first = (z * N_X + lane) * SLAB
        start = jnp.int32(0)
        for bound in bounds:
            start = jnp.where(first >= bound, bound, start)
        low = start >> PAIR_BITS
        low_of[z] = low - items
        items = items + (first >> PAIR_BITS) - low + 1
        end_of[z] = items

    @pl.loop(0, N_Z)
    def _(z):
        targets = slot_rows(code_ref[pl.ds(z, 1), :], HEAD_PAIRS, Q_ROWS)
        select_ref[z] = one_hot(N_DP * Q_ROWS, targets)
        tops_ref[z] = jnp.full((8, columns), MASKED, jnp.float32)
        sums_ref[z] = jnp.zeros((8, columns), jnp.float32)
        acc_ref[z] = jnp.zeros((HEAD_SIZE, columns), jnp.float32)
        copy_in(z).wait()
        slots = slots_ref[z].reshape(N_DP * Q_ROWS, WIDE)
        query_t = contract(slots, select_ref[z], 0, 0).astype(jnp.bfloat16)
        query_ref[z, :, : columns // 2] = query_t[:HEAD_SIZE]
        query_ref[z, :, columns // 2 :] = query_t[HEAD_SIZE:]

    in_slab = lax.broadcasted_iota(jnp.int32, (1, SLAB), 1)
    in_pair = lax.broadcasted_iota(jnp.int32, (PAIR, SLAB), 0)

    def score(item, z):
        pair = low_of[z] + item
        query_at = (z * N_X + lane) * SLAB + in_slab
        start = jnp.zeros((1, SLAB), jnp.int32)
        for bound in bounds:
            start = jnp.where(query_at >= bound, bound, start)
        at = pair * PAIR
        allowed = (in_pair >= start - at) & (in_pair <= query_at - at)
        keys = jnp.concatenate([kv_ref[2 * pair, :SLAB], kv_ref[2 * pair + 1, :SLAB]], axis=0)
        s = contract(keys, query_ref[z], 1, 0)
        tops = []
        for h in range(GROUP_HEADS):
            lanes = slice(h * SLAB, (h + 1) * SLAB)
            masked = jnp.where(allowed, s[:, lanes], MASKED)
            scores_ref[item, :, lanes] = masked
            tops.append(jnp.max(masked.reshape(PAIR // 8, 8, SLAB), axis=0))
        tops_ref[z] = jnp.maximum(tops_ref[z], jnp.concatenate(tops, axis=1))

    each_item(items, end_of, score)

    @pl.loop(0, N_Z)
    def _(z):
        shift = jnp.max(tops_ref[z], axis=0, keepdims=True) * EXP2_SCALE
        tops_ref[z] = jnp.broadcast_to(shift, (8, columns))

    def weigh(item, z):
        pair = low_of[z] + item
        weights = jnp.exp2(scores_ref[item] * EXP2_SCALE - tops_ref[z, :1])
        values_t = jnp.concatenate([kv_ref[2 * pair, SLAB:], kv_ref[2 * pair + 1, SLAB:]], axis=1)
        acc_ref[z] += contract(values_t, weights.astype(jnp.bfloat16), 1, 0)
        sums_ref[z] += jnp.sum(weights.reshape(PAIR // 8, 8, columns), axis=0)

    each_item(items, end_of, weigh)

    @pl.loop(0, N_Z)
    def _(z):
        totals = jnp.sum(sums_ref[z], axis=0, keepdims=True)
        attended_t = (acc_ref[z] * (1.0 / totals)).astype(jnp.bfloat16)
        attended_t = jnp.concatenate(
            [attended_t[:, : columns // 2], attended_t[:, columns // 2 :]], axis=0
        )
        back = contract(select_ref[z], attended_t, 1, 1).astype(jnp.bfloat16)
        out_ref[z] = back.reshape(N_DP, Q_ROWS, WIDE)
        copy_out(z).start()

    @pl.loop(0, N_Z)
    def _(z):
        copy_out(z).wait()


def unpack_kernel(targets_ref, slots_ref, out_ref):
    select = one_hot(HEAD_PAIRS * SLAB, targets_ref[...])
    for z in range(N_Z):
        slots = slots_ref[:, z].reshape(N_DP * Q_ROWS, WIDE)
        rows = contract(select, slots, 1, 0).astype(jnp.bfloat16)
        for p in range(HEAD_PAIRS):
            at = (z * HEAD_PAIRS + p) * WIDE
            out_ref[:, at : at + WIDE] = rows[p * SLAB : (p + 1) * SLAB]


def call(kernel, name, outs, specs, flops, moved, exps=0, scratch=(), vmem=VMEM_BYTES, out_space=pltpu.VMEM):
    return pl.pallas_call(
        kernel,
        name=name,
        out_shape=[jax.ShapeDtypeStruct(shape, dtype) for shape, dtype in outs],
        in_specs=[pl.BlockSpec(memory_space=s) for s in specs],
        out_specs=[pl.BlockSpec(memory_space=out_space)] * len(outs),
        scratch_shapes=scratch,
        compiler_params=pltpu.CompilerParams(vmem_limit_bytes=vmem),
        cost_estimate=pl.CostEstimate(flops=flops, bytes_accessed=moved, transcendentals=exps),
    )


def exchange(blocks):
    flat = blocks.reshape((N_DP * N_Z,) + blocks.shape[2:])
    flat = lax.all_to_all(flat, EXCHANGE, split_axis=0, concat_axis=0, tiled=True)
    return flat.reshape(blocks.shape)


def local(query, key, value, doc_lengths, send_slots, slab_source, back_pack, back_index):
    V, S, H = pltpu.VMEM, pltpu.SMEM, pl.ANY
    half, whole = jnp.bfloat16, jnp.int32
    columns = GROUP_HEADS * SLAB
    q_blocks = (N_DP, N_Z, Q_ROWS, WIDE)
    kv_blocks = (N_DP, N_Z, KV_ROWS, WIDE)
    (kv_sent,) = call(
        pack_kv_kernel,
        "pack_kv",
        [(kv_blocks, half)],
        [H, H, H, H],
        2 * 10**8,
        2 * 10**6,
        0,
        [
            V((1, 1, SLAB), whole),
            V((1, 1, SLAB), whole),
            V((2 * SLAB, KEY_VALUE_HEADS * HEAD_SIZE), half),
            pltpu.SemaphoreType.DMA((4,)),
        ],
        60 * 1024 * 1024,
    )(back_index, slab_source, key, value)
    kv_slots = exchange(kv_sent)
    own_code = back_index.reshape(1, SLAB)
    (q_sent,) = call(pack_q_kernel, "pack_q", [(q_blocks, half)], [V, V], 8 * 10**8, 3 * 10**6)(
        own_code, query
    )
    sent = send_slots.reshape(N_DP, 1, CAP)
    run = jnp.arange(HEAD_PAIRS, dtype=whole).reshape(1, HEAD_PAIRS, 1)
    targets = jnp.where(sent < SLAB, sent + run * SLAB, -1).reshape(1, N_DP * Q_ROWS)
    q_sent, kv_slots, targets = lax.optimization_barrier((q_sent, kv_slots, targets))
    q_slots = exchange(q_sent)
    group = lax.axis_index(("y", "core")).astype(whole).reshape(1)
    kv_placed, code = call(
        place_kv_kernel,
        "place_kv",
        [((N_Z, 2 * SLAB, HEAD_SIZE), half), ((N_Z, SLAB), whole)],
        [S, V],
        2 * 10**8,
        2 * 10**6,
    )(group, kv_slots)
    lane = lax.axis_index("x").astype(whole).reshape(1)
    pieces = [kv_placed] + [
        lax.ppermute(kv_placed, "x", [(x, (x + back) % N_X) for x in range(N_X)])
        for back in range(1, N_X)
    ]
    (kv_blocks_all,) = call(
        order_kv_kernel,
        "order_kv",
        [((N_Z * N_X, 2 * SLAB, HEAD_SIZE), half)],
        [S] + [V] * N_X,
        10**6,
        4 * 10**6,
    )(lane, *pieces)
    f32 = jnp.float32
    (out_sent,) = call(
        attend_kernel,
        "attend",
        [(q_blocks, half)],
        [S, S, V, pl.ANY, V],
        4 * 10**9,
        5 * 10**6,
        3 * 10**6,
        [
            V((N_Z, N_DP, Q_ROWS, WIDE), half),
            V((N_Z, N_DP, Q_ROWS, WIDE), half),
            V((N_Z, N_DP * Q_ROWS, HEAD_PAIRS * SLAB), half),
            V((N_Z, HEAD_SIZE, columns), half),
            V((MAX_ITEMS, PAIR, columns), f32),
            V((N_Z, 8, columns), f32),
            V((N_Z, 8, columns), f32),
            V((N_Z, HEAD_SIZE, columns), f32),
            S((N_Z,), whole),
            S((N_Z,), whole),
            pltpu.SemaphoreType.DMA((N_Z,)),
            pltpu.SemaphoreType.DMA((N_Z,)),
        ],
        48 * 1024 * 1024,
        pl.ANY,
    )(doc_lengths.reshape(DOCS), lane, code, q_slots, kv_blocks_all)
    out_slots = exchange(out_sent)
    (out,) = call(
        unpack_kernel,
        "unpack",
        [((SLAB, QUERY_HEADS * HEAD_SIZE), half)],
        [V, V],
        8 * 10**8,
        3 * 10**6,
    )(targets, out_slots)
    return out


def solution(mesh):
    wide = Mesh(mesh.devices.reshape(N_DP // 2, 2, N_Z, N_X), ("y", "core", "z", "x"))
    rows = P(("y", "core", "z", "x"), None)
    table = P(("y", "core"), ("z", "x"), None)
    return jax.shard_map(
        local,
        mesh=wide,
        in_specs=(rows, rows, rows, P(("y", "core"), None, None), table, table, table, table),
        out_specs=rows,
        check_vma=False,
    )
```

time: 172 us -> 168 us (0.977)
  blocking collectives: 0 us -> 51.3 us
  waiting for transfers between devices: 97.3 us -> 57.1 us
  starting transfers between devices: 41.7 us -> 34.2 us
  Pallas kernels: 26.3 us -> 19.4 us
    all_to_all x0 -> x1, blocking collectives: none -> 51.3 us  [exchange(): lax.all_to_all(flat, EXCHANGE, split_axis=0, concat_axis=0, tiled=True)]
    all_to_all x3 -> x2, waiting for transfers between devices: 78.7 us -> 34.3 us  [exchange(): lax.all_to_all(flat, EXCHANGE, split_axis=0, concat_axis=0, tiled=True)]
    all_to_all x3 -> x2, starting transfers between devices: 31.1 us -> 24.8 us  [exchange(): lax.all_to_all(flat, EXCHANGE, split_axis=0, concat_axis=0, tiled=True)]
    pallas_call x1, Pallas kernels: 17.1 us -> 12.8 us  [local(): call(attend_kernel, 'attend', [(q_blocks, half)], [S, S, V, pl.ANY, V], 4...]
    ppermute x3, waiting for transfers between devices: 18.7 us -> 22.8 us  [local(): lax.ppermute(kv_placed, 'x', [(x, (x + back) % N_X) for x in range(N_X)])]
    unnamed x19 -> x17, local copies, waits for them, and re-layouts: 5.37 us -> 4.22 us
  transfers between devices with their start and end apart: 6 -> 5, of which waited for: 6 -> 4; matrix products, arithmetic and copies ran while one was open for 1% -> 1% of each run, Pallas kernels for 2% -> 1%
where the time goes in v4:
time: 168 us; the launch traced here: 167 us
  waiting for transfers between devices  57.1 us (34%)
  blocking collectives  51.3 us (31%)
  starting transfers between devices  34.2 us (20%)
  Pallas kernels  19.4 us (12%)
  local copies, waits for them, and re-layouts  4.41 us (3%)
    all_to_all x1, blocking collectives, exchange(): lax.all_to_all(flat, EXCHANGE, split_axis=0, concat_axis=0, tiled=True)  51.3 us
    all_to_all x2, waiting for transfers between devices, exchange(): lax.all_to_all(flat, EXCHANGE, split_axis=0, concat_axis=0, tiled=True)  34.3 us
    all_to_all x2, starting transfers between devices, exchange(): lax.all_to_all(flat, EXCHANGE, split_axis=0, concat_axis=0, tiled=True)  24.8 us
    ppermute x3, waiting for transfers between devices, local(): lax.ppermute(kv_placed, 'x', [(x, (x + back) % N_X) for x in range(N_X)])  22.8 us
    pallas_call x1, Pallas kernels, local(): call(attend_kernel, 'attend', [(q_blocks, half)], [S, S, V, pl.ANY, V], 4...  12.8 us
    ppermute x3, starting transfers between devices, local(): lax.ppermute(kv_placed, 'x', [(x, (x + back) % N_X) for x in range(N_X)])  9.36 us
    unnamed x17, local copies, waits for them, and re-layouts  4.22 us
  transfers between devices with their start and end apart: 5, of which 4 were waited for; matrix products, arithmetic and copies ran while one was open for 1% of the time, Pallas kernels for 1%

profile of v4, /device:TPU:1, one launch (start us, length us, event | category | flops | bytes accessed | tf_op | source)
XLA Modules:
  0.0 167.2 jit_solution(2317226564699602485)
XLA Ops:
  0.0 2.6 %pack_kv.1 = bf16[16,8,16,256]{3,2,1,0:T(8,128)(2,1)} custom-call(s32[1,1,128]{2,1,0:T(1,128)} %code_ref.1, s32[1,1,128]{2,1,0:T(1,128)} %table_ref.1, bf16[128,1024]{1,0:T(8,128)(2,1)} %key_ref.1, bf16[128,1024]{1,0:T(8,128)(2,1)} %value_ref.1), custom_call_target="tpu_custom_call" | custom-call | flops 200000000 | bytes 2000000 | tf_op jit(solution)/shard_map/pack_kv/pallas_call | solution.py:276
  2.6 18.4 %all-to-all-start = ((bf16[128,16,256]{2,1,0:T(8,128)(2,1)}), bf16[128,16,256]{2,1,0:T(8,128)(2,1)S(1)}, u32[]{:S(2)}, u32[]{:S(2)}) async-start(bf16[128,16,256]{2,1,0:T(8,128)(2,1)} %bitcast.15), calls=%async_computation | async-start | bytes 2097152 | tf_op jit(solution)/shard_map/all_to_all | solution.py:266
  21.0 0.5 broadcast.33
  21.6 0.6 reduce.3
  22.1 0.1 reshape.87
  22.3 0.1 select_n.15.targets_ref
  22.5 1.7 %pack_q.1 = bf16[16,8,24,256]{3,2,1,0:T(8,128)(2,1)} custom-call(s32[1,128]{1,0:T(1,128)S(1)} %bitcast.13, bf16[128,4096]{1,0:T(8,128)(2,1)S(1)} %copy-done.5), custom_call_target="tpu_custom_call" | custom-call | flops 800000000 | bytes 3000000 | tf_op jit(solution)/shard_map/pack_q/pallas_call | solution.py:294
  24.2 28.9 %all-to-all-done = bf16[128,16,256]{2,1,0:T(8,128)(2,1)S(1)} async-done(((bf16[128,16,256]{2,1,0:T(8,128)(2,1)}), bf16[128,16,256]{2,1,0:T(8,128)(2,1)S(1)}, u32[]{:S(2)}, u32[]{:S(2)}) %all-to-all-start) | async-done | bytes 1048608 | tf_op jit(solution)/shard_map/all_to_all | solution.py:266
  53.1 6.4 %all-to-all-start.1 = ((bf16[128,24,256]{2,1,0:T(8,128)(2,1)}), bf16[128,24,256]{2,1,0:T(8,128)(2,1)}, u32[]{:S(2)}, u32[]{:S(2)}) async-start(bf16[128,24,256]{2,1,0:T(8,128)(2,1)} %bitcast.6), calls=%async_computation.1 | async-start | bytes 3145728 | tf_op jit(solution)/shard_map/all_to_all | solution.py:266
  59.5 0.5 place_kv.1
  60.0 4.4 %collective-permute-start.2 = (bf16[8,256,128]{2,1,0:T(8,128)(2,1)S(1)}, bf16[8,256,128]{2,1,0:T(8,128)(2,1)S(1)}, u32[]{:S(2)}, u32[]{:S(2)}) collective-permute-start(bf16[8,256,128]{2,1,0:T(8,128)(2,1)S(1)} %get-tuple-element.14.refs_0_), channel_id=1, source_target_pairs={{0,3},{1,0},{2,1},{3,2},{4,7},{5,4},{6,5},{7,6},{8,11},{9,8},{10,9... | collective-permute-start | bytes 1572872 | tf_op jit(solution)/shard_map/ppermute | solution.py:313
  64.4 2.4 %collective-permute-start.1 = (bf16[8,256,128]{2,1,0:T(8,128)(2,1)S(1)}, bf16[8,256,128]{2,1,0:T(8,128)(2,1)S(1)}, u32[]{:S(2)}, u32[]{:S(2)}) collective-permute-start(bf16[8,256,128]{2,1,0:T(8,128)(2,1)S(1)} %get-tuple-element.14.refs_0_), channel_id=1, source_target_pairs={{0,2},{1,3},{2,0},{3,1},{4,6},{5,7},{6,4},{7,5},{8,10},{9,11},{10,... | collective-permute-start | bytes 1572872 | tf_op jit(solution)/shard_map/ppermute | solution.py:313
  66.8 2.5 %collective-permute-start = (bf16[8,256,128]{2,1,0:T(8,128)(2,1)S(1)}, bf16[8,256,128]{2,1,0:T(8,128)(2,1)S(1)}, u32[]{:S(2)}, u32[]{:S(2)}) collective-permute-start(bf16[8,256,128]{2,1,0:T(8,128)(2,1)S(1)} %get-tuple-element.14.refs_0_), channel_id=1, source_target_pairs={{0,1},{1,2},{2,3},{3,0},{4,5},{5,6},{6,7},{7,4},{8,9},{9,10},{10,1... | collective-permute-start | bytes 1572872 | tf_op jit(solution)/shard_map/ppermute | solution.py:313
  69.4 17.4 %collective-permute-done.2.refs_3_ = bf16[8,256,128]{2,1,0:T(8,128)(2,1)S(1)} collective-permute-done((bf16[8,256,128]{2,1,0:T(8,128)(2,1)S(1)}, bf16[8,256,128]{2,1,0:T(8,128)(2,1)S(1)}, u32[]{:S(2)}, u32[]{:S(2)}) %collective-permute-start.2) | collective-permute-done | bytes 524320 | tf_op jit(solution)/shard_map/ppermute | solution.py:313
  86.8 0.8 copy-done
  87.6 5.4 %collective-permute-done.refs_1_ = bf16[8,256,128]{2,1,0:T(8,128)(2,1)S(1)} collective-permute-done((bf16[8,256,128]{2,1,0:T(8,128)(2,1)S(1)}, bf16[8,256,128]{2,1,0:T(8,128)(2,1)S(1)}, u32[]{:S(2)}, u32[]{:S(2)}) %collective-permute-start) | collective-permute-done | bytes 524320 | tf_op jit(solution)/shard_map/ppermute | solution.py:313
  93.0 0.8 copy-done.2
  93.8 1.0 copy-done.1
  94.8 1.0 copy-done.3
  95.9 0.1 order_kv.1.kv_ref
  96.0 5.4 %all-to-all-done.1 = bf16[128,24,256]{2,1,0:T(8,128)(2,1)} async-done(((bf16[128,24,256]{2,1,0:T(8,128)(2,1)}), bf16[128,24,256]{2,1,0:T(8,128)(2,1)}, u32[]{:S(2)}, u32[]{:S(2)}) %all-to-all-start.1) | async-done | bytes 1572896 | tf_op jit(solution)/shard_map/all_to_all | solution.py:266
  101.4 12.8 %attend.1 = bf16[16,8,24,256]{3,2,1,0:T(8,128)(2,1)S(1)} custom-call(s32[8]{0:T(128)S(1)} %bitcast.14, s32[1]{0:T(128)} %bitcast.4.lane_ref, s32[8,128]{1,0:T(8,128)S(1)} %get-tuple-element.12.code_ref, bf16[16,8,24,256]{3,2,1,0:T(8,128)(2,1)} %bitcast.7.slots_hbm, bf16[32,256,128]{2,1,0:T(8,128)(2,1)S(1)} %order_kv.1.kv_ref), custom_call_target="tpu_custom_call" | custom-call | flops 4000000000 | bytes 5000000 | tf_op jit(solution)/shard_map/attend/pallas_call | solution.py:325
  114.2 51.3 %all_to_all.15 = bf16[128,24,256]{2,1,0:T(8,128)(2,1)S(1)} all-to-all(bf16[128,24,256]{2,1,0:T(8,128)(2,1)S(1)} %bitcast.11), channel_id=1, replica_groups=mesh['y'=8,'core'=2,'z'=8,'x'=4] {'y','core','z'}, dimensions={0} | all-to-all | bytes 3145728 | tf_op jit(solution)/shard_map/all_to_all | solution.py:266
  165.5 1.7 %unpack.1 = bf16[128,4096]{1,0:T(8,128)(2,1)} custom-call(s32[1,384]{1,0:T(1,128)S(1)} %select_n.15.targets_ref, bf16[16,8,24,256]{3,2,1,0:T(8,128)(2,1)S(1)} %bitcast.12), custom_call_target="tpu_custom_call" | custom-call | flops 800000000 | bytes 3000000 | tf_op jit(solution)/shard_map/unpack/pallas_call | solution.py:351
  (16 shorter events, 0.1 us)
Async XLA Ops:
  0.0 22.4 %copy-start.4 = (s32[1,1,128]{2,1,0:T(1,128)S(1)}, s32[1,1,128]{2,1,0:T(1,128)}, u32[]{:S(2)}) copy-start(s32[1,1,128]{2,1,0:T(1,128)} %code_ref.1) | copy-start | bytes 1540
  0.0 21.6 %copy-start.7 = (s32[1,1,192]{2,1,0:T(1,128)S(1)}, s32[1,1,192]{2,1,0:T(1,128)}, u32[]{:S(2)}) copy-start(s32[1,1,192]{2,1,0:T(1,128)} %param.12) | copy-start | bytes 2308
  0.0 22.4 %copy-start.5 = (bf16[128,4096]{1,0:T(8,128)(2,1)S(1)}, bf16[128,4096]{1,0:T(8,128)(2,1)}, u32[]{:S(2)}) copy-start(bf16[128,4096]{1,0:T(8,128)(2,1)} %query_ref.1) | copy-start | bytes 3145732
  2.6 50.5 %all-to-all-start = ((bf16[128,16,256]{2,1,0:T(8,128)(2,1)}), bf16[128,16,256]{2,1,0:T(8,128)(2,1)S(1)}, u32[]{:S(2)}, u32[]{:S(2)}) async-start(bf16[128,16,256]{2,1,0:T(8,128)(2,1)} %bitcast.15), calls=%async_computation | async-start | bytes 2097152 | tf_op jit(solution)/shard_map/all_to_all | solution.py:266
  53.1 48.4 %all-to-all-start.1 = ((bf16[128,24,256]{2,1,0:T(8,128)(2,1)}), bf16[128,24,256]{2,1,0:T(8,128)(2,1)}, u32[]{:S(2)}, u32[]{:S(2)}) async-start(bf16[128,24,256]{2,1,0:T(8,128)(2,1)} %bitcast.6), calls=%async_computation.1 | async-start | bytes 3145728 | tf_op jit(solution)/shard_map/all_to_all | solution.py:266
  60.0 26.8 %collective-permute-start.2 = (bf16[8,256,128]{2,1,0:T(8,128)(2,1)S(1)}, bf16[8,256,128]{2,1,0:T(8,128)(2,1)S(1)}, u32[]{:S(2)}, u32[]{:S(2)}) collective-permute-start(bf16[8,256,128]{2,1,0:T(8,128)(2,1)S(1)} %get-tuple-element.14.refs_0_), channel_id=1, source_target_pairs={{0,3},{1,0},{2,1},{3,2},{4,7},{5,4},{6,5},{7,6},{8,11},{9,8},{10,9... | collective-permute-start | bytes 1572872 | tf_op jit(solution)/shard_map/ppermute | solution.py:313
  64.4 22.3 %collective-permute-start.1 = (bf16[8,256,128]{2,1,0:T(8,128)(2,1)S(1)}, bf16[8,256,128]{2,1,0:T(8,128)(2,1)S(1)}, u32[]{:S(2)}, u32[]{:S(2)}) collective-permute-start(bf16[8,256,128]{2,1,0:T(8,128)(2,1)S(1)} %get-tuple-element.14.refs_0_), channel_id=1, source_target_pairs={{0,2},{1,3},{2,0},{3,1},{4,6},{5,7},{6,4},{7,5},{8,10},{9,11},{10,... | collective-permute-start | bytes 1572872 | tf_op jit(solution)/shard_map/ppermute | solution.py:313
  66.8 26.1 %collective-permute-start = (bf16[8,256,128]{2,1,0:T(8,128)(2,1)S(1)}, bf16[8,256,128]{2,1,0:T(8,128)(2,1)S(1)}, u32[]{:S(2)}, u32[]{:S(2)}) collective-permute-start(bf16[8,256,128]{2,1,0:T(8,128)(2,1)S(1)} %get-tuple-element.14.refs_0_), channel_id=1, source_target_pairs={{0,1},{1,2},{2,3},{3,0},{4,5},{5,6},{6,7},{7,4},{8,9},{9,10},{10,1... | collective-permute-start | bytes 1572872 | tf_op jit(solution)/shard_map/ppermute | solution.py:313
  86.8 0.8 copy-start
  93.0 0.8 copy-start.2
  93.8 1.0 copy-start.1
  94.8 1.0 copy-start.3
  95.9 5.6 %copy-start.6 = (s32[1,1,8]{2,1,0:T(1,128)S(1)}, s32[1,1,8]{2,1,0:T(1,128)}, u32[]{:S(2)}) copy-start(s32[1,1,8]{2,1,0:T(1,128)} %param.11) | copy-start | bytes 100

commit v5 on v4

--- a/solution.py
+++ b/solution.py
@@ -23,12 +23,12 @@
 Q_ROWS = HEAD_PAIRS * CAP
 KV_ROWS = 16
 PAIR = 2 * SLAB
-PAIR_BITS = 8
+SLAB_BITS = 7
 MAX_ITEMS = 48
 STEPS = (8, 2, 1)
 EXP2_SCALE = math.log2(math.e) / math.sqrt(HEAD_SIZE)
 MASKED = -1e30
-VMEM_BYTES = 24 * 1024 * 1024
+VMEM_BYTES = 16 * 1024 * 1024
 EXCHANGE = ("y", "core", "z")
 
 
@@ -49,8 +49,12 @@
     )
 
 
+def copy_slab(slabs_ref, blocks_hbm, sems, z):
+    return pltpu.make_async_copy(slabs_ref.at[z], blocks_hbm.at[:, z], sems.at[z])
+
+
 def pack_kv_kernel(
-    code_ref, table_ref, key_ref, value_ref, out_ref, code, table, rows, sems
+    code_ref, table_ref, key_ref, value_ref, out_hbm, code, table, rows, out_ref, sems, out_sems
 ):
     copies = [
         pltpu.make_async_copy(code_ref, code, sems.at[0]),
@@ -70,7 +74,10 @@
         lanes = slice(z * HEAD_SIZE, (z + 1) * HEAD_SIZE)
         both = jnp.concatenate([rows[:SLAB, lanes], rows[SLAB:, lanes]], axis=1)
         sent = (contract(select, both, 1, 0) + codes).astype(jnp.bfloat16)
-        out_ref[:, z] = sent.reshape(N_DP, KV_ROWS, WIDE)
+        out_ref[z] = sent.reshape(N_DP, KV_ROWS, WIDE)
+        copy_slab(out_ref, out_hbm, out_sems, z).start()
+    for z in range(N_Z):
+        copy_slab(out_ref, out_hbm, out_sems, z).wait()
 
 
 def pack_q_kernel(code_ref, query_ref, out_ref):
@@ -99,14 +106,6 @@
         out_ref[z, SLAB:] = values_t.astype(jnp.bfloat16)
 
 
-def order_kv_kernel(lane_ref, *refs):
-    out_ref = refs[N_X]
-    for back, piece_ref in enumerate(refs[:N_X]):
-        x = (lane_ref[0] - back) & (N_X - 1)
-        for z in range(N_Z):
-            out_ref[z * N_X + x] = piece_ref[z]
-
-
 def each_item(items, end_of, body):
     done, slab = jnp.int32(0), jnp.int32(0)
     for size in STEPS:
@@ -128,8 +127,12 @@
     lane_ref,
     code_ref,
     slots_hbm,
+    piece_0,
+    piece_1,
+    piece_2,
+    piece_3,
+    out_hbm,
     kv_ref,
-    out_hbm,
     slots_ref,
     out_ref,
     select_ref,
@@ -142,6 +145,7 @@
     end_of,
     in_sems,
     out_sems,
+    piece_sems,
 ):
     lane = lane_ref[0]
     columns = GROUP_HEADS * SLAB
@@ -149,11 +153,15 @@
     def copy_in(z):
         return pltpu.make_async_copy(slots_hbm.at[:, z], slots_ref.at[z], in_sems.at[z])
 
-    def copy_out(z):
-        return pltpu.make_async_copy(out_ref.at[z], out_hbm.at[:, z], out_sems.at[z])
+    pieces = [
+        pltpu.make_async_copy(piece, kv_ref.at[:, (lane - back) & (N_X - 1)], piece_sems.at[back])
+        for back, piece in enumerate((piece_0, piece_1, piece_2, piece_3))
+    ]
 
     for z in range(N_Z):
         copy_in(z).start()
+    for piece in pieces:
+        piece.start()
 
     bounds = []
     total = jnp.int32(0)
@@ -167,9 +175,10 @@
         start = jnp.int32(0)
         for bound in bounds:
             start = jnp.where(first >= bound, bound, start)
-        low = start >> PAIR_BITS
-        low_of[z] = low - items
-        items = items + (first >> PAIR_BITS) - low + 1
+        block = z * N_X + lane
+        count = (block - (start >> SLAB_BITS) + 2) >> 1
+        low_of[z] = block + 1 - 2 * count - 2 * items
+        items = items + count
         end_of[z] = items
 
     @pl.loop(0, N_Z)
@@ -185,19 +194,27 @@
         query_ref[z, :, : columns // 2] = query_t[:HEAD_SIZE]
         query_ref[z, :, columns // 2 :] = query_t[HEAD_SIZE:]
 
+    for piece in pieces:
+        piece.wait()
+
+    def place(item, z):
+        block = low_of[z] + 2 * item
+        lower = jnp.maximum(block, 0)
+        return block, (lower >> 2, lower & 3), ((block + 1) >> 2, (block + 1) & 3)
+
     in_slab = lax.broadcasted_iota(jnp.int32, (1, SLAB), 1)
     in_pair = lax.broadcasted_iota(jnp.int32, (PAIR, SLAB), 0)
 
     def score(item, z):
-        pair = low_of[z] + item
+        block, one, two = place(item, z)
         query_at = (z * N_X + lane) * SLAB + in_slab
         start = jnp.zeros((1, SLAB), jnp.int32)
         for bound in bounds:
             start = jnp.where(query_at >= bound, bound, start)
-        at = pair * PAIR
+        at = block * SLAB
         allowed = (in_pair >= start - at) & (in_pair <= query_at - at)
-        keys = jnp.concatenate([kv_ref[2 * pair, :SLAB], kv_ref[2 * pair + 1, :SLAB]], axis=0)
-        s = contract(keys, query_ref[z], 1, 0)
+        keys = jnp.concatenate([kv_ref[*one, :SLAB], kv_ref[*two, :SLAB]], axis=0)
+        s = contract(keys, query_ref[z], 1, 0) * EXP2_SCALE
         tops = []
         for h in range(GROUP_HEADS):
             lanes = slice(h * SLAB, (h + 1) * SLAB)
@@ -210,13 +227,13 @@
 
     @pl.loop(0, N_Z)
     def _(z):
-        shift = jnp.max(tops_ref[z], axis=0, keepdims=True) * EXP2_SCALE
+        shift = jnp.max(tops_ref[z], axis=0, keepdims=True)
         tops_ref[z] = jnp.broadcast_to(shift, (8, columns))
 
     def weigh(item, z):
-        pair = low_of[z] + item
-        weights = jnp.exp2(scores_ref[item] * EXP2_SCALE - tops_ref[z, :1])
-        values_t = jnp.concatenate([kv_ref[2 * pair, SLAB:], kv_ref[2 * pair + 1, SLAB:]], axis=1)
+        _, one, two = place(item, z)
+        weights = jnp.exp2(scores_ref[item] - tops_ref[z, :1])
+        values_t = jnp.concatenate([kv_ref[*one, SLAB:], kv_ref[*two, SLAB:]], axis=1)
         acc_ref[z] += contract(values_t, weights.astype(jnp.bfloat16), 1, 0)
         sums_ref[z] += jnp.sum(weights.reshape(PAIR // 8, 8, columns), axis=0)
 
@@ -231,21 +248,27 @@
         )
         back = contract(select_ref[z], attended_t, 1, 1).astype(jnp.bfloat16)
         out_ref[z] = back.reshape(N_DP, Q_ROWS, WIDE)
-        copy_out(z).start()
+        copy_slab(out_ref, out_hbm, out_sems, z).start()
 
     @pl.loop(0, N_Z)
     def _(z):
-        copy_out(z).wait()
-
-
-def unpack_kernel(targets_ref, slots_ref, out_ref):
+        copy_slab(out_ref, out_hbm, out_sems, z).wait()
+
+
+def unpack_kernel(targets_ref, slots_ref, out_hbm, out_ref, sems):
+    def copy_out(z):
+        lanes = pl.ds(z * HEAD_PAIRS * WIDE, HEAD_PAIRS * WIDE)
+        return pltpu.make_async_copy(out_ref.at[z], out_hbm.at[:, lanes], sems.at[z])
+
     select = one_hot(HEAD_PAIRS * SLAB, targets_ref[...])
     for z in range(N_Z):
         slots = slots_ref[:, z].reshape(N_DP * Q_ROWS, WIDE)
         rows = contract(select, slots, 1, 0).astype(jnp.bfloat16)
         for p in range(HEAD_PAIRS):
-            at = (z * HEAD_PAIRS + p) * WIDE
-            out_ref[:, at : at + WIDE] = rows[p * SLAB : (p + 1) * SLAB]
+            out_ref[z, :, p * WIDE : (p + 1) * WIDE] = rows[p * SLAB : (p + 1) * SLAB]
+        copy_out(z).start()
+    for z in range(N_Z):
+        copy_out(z).wait()
 
 
 def call(kernel, name, outs, specs, flops, moved, exps=0, scratch=(), vmem=VMEM_BYTES, out_space=pltpu.VMEM):
@@ -285,9 +308,12 @@
             V((1, 1, SLAB), whole),
             V((1, 1, SLAB), whole),
             V((2 * SLAB, KEY_VALUE_HEADS * HEAD_SIZE), half),
+            V((N_Z, N_DP, KV_ROWS, WIDE), half),
             pltpu.SemaphoreType.DMA((4,)),
+            pltpu.SemaphoreType.DMA((N_Z,)),
         ],
         60 * 1024 * 1024,
+        pl.ANY,
     )(back_index, slab_source, key, value)
     kv_slots = exchange(kv_sent)
     own_code = back_index.reshape(1, SLAB)
@@ -313,24 +339,17 @@
         lax.ppermute(kv_placed, "x", [(x, (x + back) % N_X) for x in range(N_X)])
         for back in range(1, N_X)
     ]
-    (kv_blocks_all,) = call(
-        order_kv_kernel,
-        "order_kv",
-        [((N_Z * N_X, 2 * SLAB, HEAD_SIZE), half)],
-        [S] + [V] * N_X,
-        10**6,
-        4 * 10**6,
-    )(lane, *pieces)
     f32 = jnp.float32
     (out_sent,) = call(
         attend_kernel,
         "attend",
         [(q_blocks, half)],
-        [S, S, V, pl.ANY, V],
+        [S, S, V] + [pl.ANY] * (1 + N_X),
         4 * 10**9,
         5 * 10**6,
         3 * 10**6,
         [
+            V((N_Z, N_X, 2 * SLAB, HEAD_SIZE), half),
             V((N_Z, N_DP, Q_ROWS, WIDE), half),
             V((N_Z, N_DP, Q_ROWS, WIDE), half),
             V((N_Z, N_DP * Q_ROWS, HEAD_PAIRS * SLAB), half),
@@ -343,10 +362,11 @@
             S((N_Z,), whole),
             pltpu.SemaphoreType.DMA((N_Z,)),
             pltpu.SemaphoreType.DMA((N_Z,)),
+            pltpu.SemaphoreType.DMA((N_X,)),
         ],
-        48 * 1024 * 1024,
+        40 * 1024 * 1024,
         pl.ANY,
-    )(doc_lengths.reshape(DOCS), lane, code, q_slots, kv_blocks_all)
+    )(doc_lengths.reshape(DOCS), lane, code, q_slots, *pieces)
     out_slots = exchange(out_sent)
     (out,) = call(
         unpack_kernel,
@@ -355,6 +375,10 @@
         [V, V],
         8 * 10**8,
         3 * 10**6,
+        0,
+        [V((N_Z, SLAB, HEAD_PAIRS * WIDE), half), pltpu.SemaphoreType.DMA((N_Z,))],
+        VMEM_BYTES,
+        pl.ANY,
     )(targets, out_slots)
     return out
 

time: 168 us -> 164 us (0.976)
  waiting for transfers between devices: 57.1 us -> 61.9 us
  blocking collectives: 51.3 us -> 48.3 us
  local copies, waits for them, and re-layouts: 4.41 us -> 1.89 us
  Pallas kernels: 19.4 us -> 17.2 us
    all_to_all x2, waiting for transfers between devices: 34.3 us -> 38.2 us  [exchange(): lax.all_to_all(flat, EXCHANGE, split_axis=0, concat_axis=0, tiled=True)]
    all_to_all x1, blocking collectives: 51.3 us -> 48.3 us  [exchange(): lax.all_to_all(flat, EXCHANGE, split_axis=0, concat_axis=0, tiled=True)]
    unnamed x17 -> x11, local copies, waits for them, and re-layouts: 4.22 us -> 1.7 us
    pallas_call x2 -> x1, Pallas kernels: 12.9 us -> 12.2 us  [local(): call(attend_kernel, 'attend', [(q_blocks, half)], [S, S, V] + [pl.ANY] *...]
  transfers between devices with their start and end apart: 5 -> 5, of which waited for: 4 -> 5; matrix products, arithmetic and copies ran while one was open for 1% -> 1% of each run, Pallas kernels for 1% -> 1%
where the time goes in v5:
time: 164 us; the launch traced here: 163 us
  waiting for transfers between devices  61.9 us (38%)
  blocking collectives  48.3 us (29%)
  starting transfers between devices  33.2 us (20%)
  Pallas kernels  17.2 us (10%)
  local copies, waits for them, and re-layouts  1.89 us (1%)
    all_to_all x1, blocking collectives, exchange(): lax.all_to_all(flat, EXCHANGE, split_axis=0, concat_axis=0, tiled=True)  48.3 us
    all_to_all x2, waiting for transfers between devices, exchange(): lax.all_to_all(flat, EXCHANGE, split_axis=0, concat_axis=0, tiled=True)  38.2 us
    all_to_all x2, starting transfers between devices, exchange(): lax.all_to_all(flat, EXCHANGE, split_axis=0, concat_axis=0, tiled=True)  23.9 us
    ppermute x3, waiting for transfers between devices, local(): lax.ppermute(kv_placed, 'x', [(x, (x + back) % N_X) for x in range(N_X)])  23.6 us
    pallas_call x1, Pallas kernels, local(): call(attend_kernel, 'attend', [(q_blocks, half)], [S, S, V] + [pl.ANY] *...  12.2 us
    ppermute x3, starting transfers between devices, local(): lax.ppermute(kv_placed, 'x', [(x, (x + back) % N_X) for x in range(N_X)])  9.33 us
  transfers between devices with their start and end apart: 5, of which 5 were waited for; matrix products, arithmetic and copies ran while one was open for 1% of the time, Pallas kernels for 1%

profile of v5, /device:TPU:1, one launch (start us, length us, event | category | flops | bytes accessed | tf_op | source)
XLA Modules:
  0.0 163.3 jit_solution(2299953396852407604)
XLA Ops:
  0.0 2.4 %pack_kv.1 = bf16[16,8,16,256]{3,2,1,0:T(8,128)(2,1)} custom-call(s32[1,1,128]{2,1,0:T(1,128)} %code_ref.1, s32[1,1,128]{2,1,0:T(1,128)} %table_ref.1, bf16[128,1024]{1,0:T(8,128)(2,1)} %key_ref.1, bf16[128,1024]{1,0:T(8,128)(2,1)} %value_ref.1), custom_call_target="tpu_custom_call" | custom-call | flops 200000000 | bytes 2000000 | tf_op jit(solution)/shard_map/pack_kv/pallas_call | solution.py:299
  2.4 18.4 %all-to-all-start = ((bf16[128,16,256]{2,1,0:T(8,128)(2,1)}), bf16[128,16,256]{2,1,0:T(8,128)(2,1)S(1)}, u32[]{:S(2)}, u32[]{:S(2)}) async-start(bf16[128,16,256]{2,1,0:T(8,128)(2,1)} %bitcast.17), calls=%async_computation | async-start | bytes 2097152 | tf_op jit(solution)/shard_map/all_to_all | solution.py:289
  20.9 0.5 broadcast.33
  21.4 0.0 copy-done.4
  21.4 0.7 reduce.3
  22.1 0.1 reshape.87
  22.2 0.1 add_select_fusion
  22.3 0.1 select_n.15.targets_ref
  22.4 0.0 copy-done.1
  22.4 0.6 pack_q.1
  23.0 1.1 copy-done
  24.1 28.8 %all-to-all-done = bf16[128,16,256]{2,1,0:T(8,128)(2,1)S(1)} async-done(((bf16[128,16,256]{2,1,0:T(8,128)(2,1)}), bf16[128,16,256]{2,1,0:T(8,128)(2,1)S(1)}, u32[]{:S(2)}, u32[]{:S(2)}) %all-to-all-start) | async-done | bytes 1048608 | tf_op jit(solution)/shard_map/all_to_all | solution.py:289
  52.9 5.5 %all-to-all-start.1 = ((bf16[128,24,256]{2,1,0:T(8,128)(2,1)}), bf16[128,24,256]{2,1,0:T(8,128)(2,1)S(1)}, u32[]{:S(2)}, u32[]{:S(2)}) async-start(bf16[128,24,256]{2,1,0:T(8,128)(2,1)} %bitcast.12), calls=%async_computation.1 | async-start | bytes 3145728 | tf_op jit(solution)/shard_map/all_to_all | solution.py:289
  58.4 0.5 place_kv.1
  58.9 4.4 %collective-permute-start.2 = (bf16[8,256,128]{2,1,0:T(8,128)(2,1)S(1)}, bf16[8,256,128]{2,1,0:T(8,128)(2,1)S(1)}, u32[]{:S(2)}, u32[]{:S(2)}) collective-permute-start(bf16[8,256,128]{2,1,0:T(8,128)(2,1)S(1)} %get-tuple-element.14.piece_0), channel_id=1, source_target_pairs={{0,3},{1,0},{2,1},{3,2},{4,7},{5,4},{6,5},{7,6},{8,11},{9,8},{10,9... | collective-permute-start | bytes 1572872 | tf_op jit(solution)/shard_map/ppermute | solution.py:339
  63.3 2.4 %collective-permute-start.1 = (bf16[8,256,128]{2,1,0:T(8,128)(2,1)S(1)}, bf16[8,256,128]{2,1,0:T(8,128)(2,1)S(1)}, u32[]{:S(2)}, u32[]{:S(2)}) collective-permute-start(bf16[8,256,128]{2,1,0:T(8,128)(2,1)S(1)} %get-tuple-element.14.piece_0), channel_id=1, source_target_pairs={{0,2},{1,3},{2,0},{3,1},{4,6},{5,7},{6,4},{7,5},{8,10},{9,11},{10,... | collective-permute-start | bytes 1572872 | tf_op jit(solution)/shard_map/ppermute | solution.py:339
  65.7 2.5 %collective-permute-start = (bf16[8,256,128]{2,1,0:T(8,128)(2,1)S(1)}, bf16[8,256,128]{2,1,0:T(8,128)(2,1)}, u32[]{:S(2)}, u32[]{:S(2)}) collective-permute-start(bf16[8,256,128]{2,1,0:T(8,128)(2,1)S(1)} %get-tuple-element.14.piece_0), channel_id=1, source_target_pairs={{0,1},{1,2},{2,3},{3,0},{4,5},{5,6},{6,7},{7,4},{8,9},{9,10},{10,1... | collective-permute-start | bytes 1572872 | tf_op jit(solution)/shard_map/ppermute | solution.py:339
  68.3 6.4 %collective-permute-done.2.piece_3 = bf16[8,256,128]{2,1,0:T(8,128)(2,1)S(1)} collective-permute-done((bf16[8,256,128]{2,1,0:T(8,128)(2,1)S(1)}, bf16[8,256,128]{2,1,0:T(8,128)(2,1)S(1)}, u32[]{:S(2)}, u32[]{:S(2)}) %collective-permute-start.2) | collective-permute-done | bytes 524320 | tf_op jit(solution)/shard_map/ppermute | solution.py:339
  74.6 4.5 %collective-permute-done.1.piece_2 = bf16[8,256,128]{2,1,0:T(8,128)(2,1)S(1)} collective-permute-done((bf16[8,256,128]{2,1,0:T(8,128)(2,1)S(1)}, bf16[8,256,128]{2,1,0:T(8,128)(2,1)S(1)}, u32[]{:S(2)}, u32[]{:S(2)}) %collective-permute-start.1) | collective-permute-done | bytes 524320 | tf_op jit(solution)/shard_map/ppermute | solution.py:339
  79.2 12.7 %collective-permute-done.piece_1 = bf16[8,256,128]{2,1,0:T(8,128)(2,1)} collective-permute-done((bf16[8,256,128]{2,1,0:T(8,128)(2,1)S(1)}, bf16[8,256,128]{2,1,0:T(8,128)(2,1)}, u32[]{:S(2)}, u32[]{:S(2)}) %collective-permute-start) | collective-permute-done | bytes 524320 | tf_op jit(solution)/shard_map/ppermute | solution.py:339
  91.9 9.4 %all-to-all-done.1 = bf16[128,24,256]{2,1,0:T(8,128)(2,1)S(1)} async-done(((bf16[128,24,256]{2,1,0:T(8,128)(2,1)}), bf16[128,24,256]{2,1,0:T(8,128)(2,1)S(1)}, u32[]{:S(2)}, u32[]{:S(2)}) %all-to-all-start.1) | async-done | bytes 1572896 | tf_op jit(solution)/shard_map/all_to_all | solution.py:289
  101.3 12.2 %attend.1 = bf16[16,8,24,256]{3,2,1,0:T(8,128)(2,1)S(1)} custom-call(s32[8]{0:T(128)S(1)} %bitcast.16, s32[1]{0:T(128)} %bitcast.4.lane_ref, s32[8,128]{1,0:T(8,128)S(1)} %get-tuple-element.12.code_ref, bf16[16,8,24,256]{3,2,1,0:T(8,128)(2,1)S(1)} %bitcast.11, bf16[8,256,128]{2,1,0:T(8,128)(2,1)S(1)} %get-tuple-element.14.piece_0, ...), custom_call_target="tpu_custom_call" | custom-call | flops 4000000000 | bytes 5000000 | tf_op jit(solution)/shard_map/attend/pallas_call | solution.py:343
  113.5 48.3 %all_to_all.15 = bf16[128,24,256]{2,1,0:T(8,128)(2,1)S(1)} all-to-all(bf16[128,24,256]{2,1,0:T(8,128)(2,1)S(1)} %bitcast.13), channel_id=1, replica_groups=mesh['y'=8,'core'=2,'z'=8,'x'=4] {'y','core','z'}, dimensions={0} | all-to-all | bytes 3145728 | tf_op jit(solution)/shard_map/all_to_all | solution.py:289
  161.8 1.5 unpack.1
  (9 shorter events, 0.0 us)
Async XLA Ops:
  0.0 22.4 %copy-start.1 = (s32[1,1,128]{2,1,0:T(1,128)S(1)}, s32[1,1,128]{2,1,0:T(1,128)}, u32[]{:S(2)}) copy-start(s32[1,1,128]{2,1,0:T(1,128)} %code_ref.1) | copy-start | bytes 1540
  0.0 21.4 %copy-start.4 = (s32[1,1,192]{2,1,0:T(1,128)S(1)}, s32[1,1,192]{2,1,0:T(1,128)}, u32[]{:S(2)}) copy-start(s32[1,1,192]{2,1,0:T(1,128)} %param.12) | copy-start | bytes 2308
  0.0 22.4 %copy-start.2 = (bf16[128,4096]{1,0:T(8,128)(2,1)S(1)}, bf16[128,4096]{1,0:T(8,128)(2,1)}, u32[]{:S(2)}) copy-start(bf16[128,4096]{1,0:T(8,128)(2,1)} %query_ref.1) | copy-start | bytes 3145732
  2.4 50.5 %all-to-all-start = ((bf16[128,16,256]{2,1,0:T(8,128)(2,1)}), bf16[128,16,256]{2,1,0:T(8,128)(2,1)S(1)}, u32[]{:S(2)}, u32[]{:S(2)}) async-start(bf16[128,16,256]{2,1,0:T(8,128)(2,1)} %bitcast.17), calls=%async_computation | async-start | bytes 2097152 | tf_op jit(solution)/shard_map/all_to_all | solution.py:289
  23.0 1.2 copy-start
  52.9 48.4 %copy-start.3 = (s32[1,1,8]{2,1,0:T(1,128)S(1)}, s32[1,1,8]{2,1,0:T(1,128)}, u32[]{:S(2)}) copy-start(s32[1,1,8]{2,1,0:T(1,128)} %param.11) | copy-start | bytes 100
  52.9 48.4 %all-to-all-start.1 = ((bf16[128,24,256]{2,1,0:T(8,128)(2,1)}), bf16[128,24,256]{2,1,0:T(8,128)(2,1)S(1)}, u32[]{:S(2)}, u32[]{:S(2)}) async-start(bf16[128,24,256]{2,1,0:T(8,128)(2,1)} %bitcast.12), calls=%async_computation.1 | async-start | bytes 3145728 | tf_op jit(solution)/shard_map/all_to_all | solution.py:289
  58.9 15.7 %collective-permute-start.2 = (bf16[8,256,128]{2,1,0:T(8,128)(2,1)S(1)}, bf16[8,256,128]{2,1,0:T(8,128)(2,1)S(1)}, u32[]{:S(2)}, u32[]{:S(2)}) collective-permute-start(bf16[8,256,128]{2,1,0:T(8,128)(2,1)S(1)} %get-tuple-element.14.piece_0), channel_id=1, source_target_pairs={{0,3},{1,0},{2,1},{3,2},{4,7},{5,4},{6,5},{7,6},{8,11},{9,8},{10,9... | collective-permute-start | bytes 1572872 | tf_op jit(solution)/shard_map/ppermute | solution.py:339
  63.3 15.9 %collective-permute-start.1 = (bf16[8,256,128]{2,1,0:T(8,128)(2,1)S(1)}, bf16[8,256,128]{2,1,0:T(8,128)(2,1)S(1)}, u32[]{:S(2)}, u32[]{:S(2)}) collective-permute-start(bf16[8,256,128]{2,1,0:T(8,128)(2,1)S(1)} %get-tuple-element.14.piece_0), channel_id=1, source_target_pairs={{0,2},{1,3},{2,0},{3,1},{4,6},{5,7},{6,4},{7,5},{8,10},{9,11},{10,... | collective-permute-start | bytes 1572872 | tf_op jit(solution)/shard_map/ppermute | solution.py:339
  65.7 26.1 %collective-permute-start = (bf16[8,256,128]{2,1,0:T(8,128)(2,1)S(1)}, bf16[8,256,128]{2,1,0:T(8,128)(2,1)}, u32[]{:S(2)}, u32[]{:S(2)}) collective-permute-start(bf16[8,256,128]{2,1,0:T(8,128)(2,1)S(1)} %get-tuple-element.14.piece_0), channel_id=1, source_target_pairs={{0,1},{1,2},{2,3},{3,0},{4,5},{5,6},{6,7},{7,4},{8,9},{9,10},{10,1... | collective-permute-start | bytes 1572872 | tf_op jit(solution)/shard_map/ppermute | solution.py:339

commit v6 on v5

--- a/solution.py
+++ b/solution.py
@@ -25,7 +25,7 @@
 PAIR = 2 * SLAB
 SLAB_BITS = 7
 MAX_ITEMS = 48
-STEPS = (8, 2, 1)
+STEPS = (16, 8, 4, 2, 1)
 EXP2_SCALE = math.log2(math.e) / math.sqrt(HEAD_SIZE)
 MASKED = -1e30
 VMEM_BYTES = 16 * 1024 * 1024
@@ -64,12 +64,14 @@
     ]
     for copy in copies:
         copy.start()
-    for copy in copies:
+    for copy in copies[:2]:
         copy.wait()
     select = one_hot(N_DP * KV_ROWS, slot_rows(code[0], 1, KV_ROWS))
     codes = table[0].astype(jnp.float32)
     at = lax.broadcasted_iota(jnp.int32, (N_DP * KV_ROWS, WIDE), 0) & (KV_ROWS - 1)
     codes = jnp.where(at >= CAP, jnp.concatenate([codes, codes], axis=1), 0.0)
+    for copy in copies[2:]:
+        copy.wait()
     for z in range(N_Z):
         lanes = slice(z * HEAD_SIZE, (z + 1) * HEAD_SIZE)
         both = jnp.concatenate([rows[:SLAB, lanes], rows[SLAB:, lanes]], axis=1)

time: 164 us -> 164 us (level)
  no operation moved by 1% of the time
where the time goes in v6:
time: 164 us
  waiting for transfers between devices  61.9 us (38%)
  blocking collectives  49.6 us (30%)
  starting transfers between devices  33.2 us (20%)
  Pallas kernels  16.3 us (10%)
  local copies, waits for them, and re-layouts  1.89 us (1%)
    all_to_all x1, blocking collectives, exchange(): lax.all_to_all(flat, EXCHANGE, split_axis=0, concat_axis=0, tiled=True)  49.6 us
    all_to_all x2, waiting for transfers between devices, exchange(): lax.all_to_all(flat, EXCHANGE, split_axis=0, concat_axis=0, tiled=True)  38.2 us
    all_to_all x2, starting transfers between devices, exchange(): lax.all_to_all(flat, EXCHANGE, split_axis=0, concat_axis=0, tiled=True)  23.9 us
    ppermute x3, waiting for transfers between devices, local(): lax.ppermute(kv_placed, 'x', [(x, (x + back) % N_X) for x in range(N_X)])  23.6 us
    pallas_call x1, Pallas kernels, local(): call(attend_kernel, 'attend', [(q_blocks, half)], [S, S, V] + [pl.ANY] *...  11.4 us
    ppermute x3, starting transfers between devices, local(): lax.ppermute(kv_placed, 'x', [(x, (x + back) % N_X) for x in range(N_X)])  9.33 us
  transfers between devices with their start and end apart: 5, of which 5 were waited for; matrix products, arithmetic and copies ran while one was open for 1% of the time, Pallas kernels for 1%

profile of v6, /device:TPU:1, one launch (start us, length us, event | category | flops | bytes accessed | tf_op | source)
XLA Modules:
  0.0 163.9 jit_solution(11102064723793879017)
XLA Ops:
  0.0 2.4 %pack_kv.1 = bf16[16,8,16,256]{3,2,1,0:T(8,128)(2,1)} custom-call(s32[1,1,128]{2,1,0:T(1,128)} %code_ref.1, s32[1,1,128]{2,1,0:T(1,128)} %table_ref.1, bf16[128,1024]{1,0:T(8,128)(2,1)} %key_ref.1, bf16[128,1024]{1,0:T(8,128)(2,1)} %value_ref.1), custom_call_target="tpu_custom_call" | custom-call | flops 200000000 | bytes 2000000 | tf_op jit(solution)/shard_map/pack_kv/pallas_call | solution.py:301
  2.4 18.4 %all-to-all-start = ((bf16[128,16,256]{2,1,0:T(8,128)(2,1)}), bf16[128,16,256]{2,1,0:T(8,128)(2,1)S(1)}, u32[]{:S(2)}, u32[]{:S(2)}) async-start(bf16[128,16,256]{2,1,0:T(8,128)(2,1)} %bitcast.17), calls=%async_computation | async-start | bytes 2097152 | tf_op jit(solution)/shard_map/all_to_all | solution.py:291
  20.9 0.5 broadcast.33
  21.4 0.7 reduce.3
  22.1 0.1 reshape.87
  22.2 0.1 add_select_fusion
  22.3 0.1 select_n.15.targets_ref
  22.4 0.6 pack_q.1
  23.0 0.0 copy-start
  23.0 1.1 copy-done
  24.1 28.8 %all-to-all-done = bf16[128,16,256]{2,1,0:T(8,128)(2,1)S(1)} async-done(((bf16[128,16,256]{2,1,0:T(8,128)(2,1)}), bf16[128,16,256]{2,1,0:T(8,128)(2,1)S(1)}, u32[]{:S(2)}, u32[]{:S(2)}) %all-to-all-start) | async-done | bytes 1048608 | tf_op jit(solution)/shard_map/all_to_all | solution.py:291
  52.9 5.5 %all-to-all-start.1 = ((bf16[128,24,256]{2,1,0:T(8,128)(2,1)}), bf16[128,24,256]{2,1,0:T(8,128)(2,1)S(1)}, u32[]{:S(2)}, u32[]{:S(2)}) async-start(bf16[128,24,256]{2,1,0:T(8,128)(2,1)} %bitcast.12), calls=%async_computation.1 | async-start | bytes 3145728 | tf_op jit(solution)/shard_map/all_to_all | solution.py:291
  58.4 0.5 place_kv.1
  58.9 4.4 %collective-permute-start.2 = (bf16[8,256,128]{2,1,0:T(8,128)(2,1)S(1)}, bf16[8,256,128]{2,1,0:T(8,128)(2,1)S(1)}, u32[]{:S(2)}, u32[]{:S(2)}) collective-permute-start(bf16[8,256,128]{2,1,0:T(8,128)(2,1)S(1)} %get-tuple-element.14.piece_0), channel_id=1, source_target_pairs={{0,3},{1,0},{2,1},{3,2},{4,7},{5,4},{6,5},{7,6},{8,11},{9,8},{10,9... | collective-permute-start | bytes 1572872 | tf_op jit(solution)/shard_map/ppermute | solution.py:341
  63.3 2.4 %collective-permute-start.1 = (bf16[8,256,128]{2,1,0:T(8,128)(2,1)S(1)}, bf16[8,256,128]{2,1,0:T(8,128)(2,1)S(1)}, u32[]{:S(2)}, u32[]{:S(2)}) collective-permute-start(bf16[8,256,128]{2,1,0:T(8,128)(2,1)S(1)} %get-tuple-element.14.piece_0), channel_id=1, source_target_pairs={{0,2},{1,3},{2,0},{3,1},{4,6},{5,7},{6,4},{7,5},{8,10},{9,11},{10,... | collective-permute-start | bytes 1572872 | tf_op jit(solution)/shard_map/ppermute | solution.py:341
  65.7 2.5 %collective-permute-start = (bf16[8,256,128]{2,1,0:T(8,128)(2,1)S(1)}, bf16[8,256,128]{2,1,0:T(8,128)(2,1)}, u32[]{:S(2)}, u32[]{:S(2)}) collective-permute-start(bf16[8,256,128]{2,1,0:T(8,128)(2,1)S(1)} %get-tuple-element.14.piece_0), channel_id=1, source_target_pairs={{0,1},{1,2},{2,3},{3,0},{4,5},{5,6},{6,7},{7,4},{8,9},{9,10},{10,1... | collective-permute-start | bytes 1572872 | tf_op jit(solution)/shard_map/ppermute | solution.py:341
  68.3 6.4 %collective-permute-done.2.piece_3 = bf16[8,256,128]{2,1,0:T(8,128)(2,1)S(1)} collective-permute-done((bf16[8,256,128]{2,1,0:T(8,128)(2,1)S(1)}, bf16[8,256,128]{2,1,0:T(8,128)(2,1)S(1)}, u32[]{:S(2)}, u32[]{:S(2)}) %collective-permute-start.2) | collective-permute-done | bytes 524320 | tf_op jit(solution)/shard_map/ppermute | solution.py:341
  74.6 4.5 %collective-permute-done.1.piece_2 = bf16[8,256,128]{2,1,0:T(8,128)(2,1)S(1)} collective-permute-done((bf16[8,256,128]{2,1,0:T(8,128)(2,1)S(1)}, bf16[8,256,128]{2,1,0:T(8,128)(2,1)S(1)}, u32[]{:S(2)}, u32[]{:S(2)}) %collective-permute-start.1) | collective-permute-done | bytes 524320 | tf_op jit(solution)/shard_map/ppermute | solution.py:341
  79.2 12.7 %collective-permute-done.piece_1 = bf16[8,256,128]{2,1,0:T(8,128)(2,1)} collective-permute-done((bf16[8,256,128]{2,1,0:T(8,128)(2,1)S(1)}, bf16[8,256,128]{2,1,0:T(8,128)(2,1)}, u32[]{:S(2)}, u32[]{:S(2)}) %collective-permute-start) | collective-permute-done | bytes 524320 | tf_op jit(solution)/shard_map/ppermute | solution.py:341
  91.9 9.4 %all-to-all-done.1 = bf16[128,24,256]{2,1,0:T(8,128)(2,1)S(1)} async-done(((bf16[128,24,256]{2,1,0:T(8,128)(2,1)}), bf16[128,24,256]{2,1,0:T(8,128)(2,1)S(1)}, u32[]{:S(2)}, u32[]{:S(2)}) %all-to-all-start.1) | async-done | bytes 1572896 | tf_op jit(solution)/shard_map/all_to_all | solution.py:291
  101.3 0.0 copy-done.3
  101.3 11.4 %attend.1 = bf16[16,8,24,256]{3,2,1,0:T(8,128)(2,1)S(1)} custom-call(s32[8]{0:T(128)S(1)} %bitcast.16, s32[1]{0:T(128)} %bitcast.4.lane_ref, s32[8,128]{1,0:T(8,128)S(1)} %get-tuple-element.12.code_ref, bf16[16,8,24,256]{3,2,1,0:T(8,128)(2,1)S(1)} %bitcast.11, bf16[8,256,128]{2,1,0:T(8,128)(2,1)S(1)} %get-tuple-element.14.piece_0, ...), custom_call_target="tpu_custom_call" | custom-call | flops 4000000000 | bytes 5000000 | tf_op jit(solution)/shard_map/attend/pallas_call | solution.py:345
  112.7 49.6 %all_to_all.15 = bf16[128,24,256]{2,1,0:T(8,128)(2,1)S(1)} all-to-all(bf16[128,24,256]{2,1,0:T(8,128)(2,1)S(1)} %bitcast.13), channel_id=1, replica_groups=mesh['y'=8,'core'=2,'z'=8,'x'=4] {'y','core','z'}, dimensions={0} | all-to-all | bytes 3145728 | tf_op jit(solution)/shard_map/all_to_all | solution.py:291
  162.3 1.5 unpack.1
  (9 shorter events, 0.0 us)
Async XLA Ops:
  0.0 22.4 %copy-start.1 = (s32[1,1,128]{2,1,0:T(1,128)S(1)}, s32[1,1,128]{2,1,0:T(1,128)}, u32[]{:S(2)}) copy-start(s32[1,1,128]{2,1,0:T(1,128)} %code_ref.1) | copy-start | bytes 1540
  0.0 21.4 %copy-start.4 = (s32[1,1,192]{2,1,0:T(1,128)S(1)}, s32[1,1,192]{2,1,0:T(1,128)}, u32[]{:S(2)}) copy-start(s32[1,1,192]{2,1,0:T(1,128)} %param.12) | copy-start | bytes 2308
  0.0 22.4 %copy-start.2 = (bf16[128,4096]{1,0:T(8,128)(2,1)S(1)}, bf16[128,4096]{1,0:T(8,128)(2,1)}, u32[]{:S(2)}) copy-start(bf16[128,4096]{1,0:T(8,128)(2,1)} %query_ref.1) | copy-start | bytes 3145732
  2.4 50.5 %all-to-all-start = ((bf16[128,16,256]{2,1,0:T(8,128)(2,1)}), bf16[128,16,256]{2,1,0:T(8,128)(2,1)S(1)}, u32[]{:S(2)}, u32[]{:S(2)}) async-start(bf16[128,16,256]{2,1,0:T(8,128)(2,1)} %bitcast.17), calls=%async_computation | async-start | bytes 2097152 | tf_op jit(solution)/shard_map/all_to_all | solution.py:291
  23.0 1.2 copy-start
  52.9 48.4 %copy-start.3 = (s32[1,1,8]{2,1,0:T(1,128)S(1)}, s32[1,1,8]{2,1,0:T(1,128)}, u32[]{:S(2)}) copy-start(s32[1,1,8]{2,1,0:T(1,128)} %param.11) | copy-start | bytes 100
  52.9 48.4 %all-to-all-start.1 = ((bf16[128,24,256]{2,1,0:T(8,128)(2,1)}), bf16[128,24,256]{2,1,0:T(8,128)(2,1)S(1)}, u32[]{:S(2)}, u32[]{:S(2)}) async-start(bf16[128,24,256]{2,1,0:T(8,128)(2,1)} %bitcast.12), calls=%async_computation.1 | async-start | bytes 3145728 | tf_op jit(solution)/shard_map/all_to_all | solution.py:291
  58.9 15.7 %collective-permute-start.2 = (bf16[8,256,128]{2,1,0:T(8,128)(2,1)S(1)}, bf16[8,256,128]{2,1,0:T(8,128)(2,1)S(1)}, u32[]{:S(2)}, u32[]{:S(2)}) collective-permute-start(bf16[8,256,128]{2,1,0:T(8,128)(2,1)S(1)} %get-tuple-element.14.piece_0), channel_id=1, source_target_pairs={{0,3},{1,0},{2,1},{3,2},{4,7},{5,4},{6,5},{7,6},{8,11},{9,8},{10,9... | collective-permute-start | bytes 1572872 | tf_op jit(solution)/shard_map/ppermute | solution.py:341
  63.3 15.9 %collective-permute-start.1 = (bf16[8,256,128]{2,1,0:T(8,128)(2,1)S(1)}, bf16[8,256,128]{2,1,0:T(8,128)(2,1)S(1)}, u32[]{:S(2)}, u32[]{:S(2)}) collective-permute-start(bf16[8,256,128]{2,1,0:T(8,128)(2,1)S(1)} %get-tuple-element.14.piece_0), channel_id=1, source_target_pairs={{0,2},{1,3},{2,0},{3,1},{4,6},{5,7},{6,4},{7,5},{8,10},{9,11},{10,... | collective-permute-start | bytes 1572872 | tf_op jit(solution)/shard_map/ppermute | solution.py:341
  65.7 26.1 %collective-permute-start = (bf16[8,256,128]{2,1,0:T(8,128)(2,1)S(1)}, bf16[8,256,128]{2,1,0:T(8,128)(2,1)}, u32[]{:S(2)}, u32[]{:S(2)}) collective-permute-start(bf16[8,256,128]{2,1,0:T(8,128)(2,1)S(1)} %get-tuple-element.14.piece_0), channel_id=1, source_target_pairs={{0,1},{1,2},{2,3},{3,0},{4,5},{5,6},{6,7},{7,4},{8,9},{9,10},{10,1... | collective-permute-start | bytes 1572872 | tf_op jit(solution)/shard_map/ppermute | solution.py:341

commit v7 on v5

--- a/solution.py
+++ b/solution.py
@@ -126,15 +126,13 @@
     lengths_ref,
     lane_ref,
     code_ref,
-    slots_hbm,
+    slots_ref,
     piece_0,
     piece_1,
     piece_2,
     piece_3,
-    out_hbm,
+    out_ref,
     kv_ref,
-    slots_ref,
-    out_ref,
     select_ref,
     query_ref,
     scores_ref,
@@ -143,23 +141,16 @@
     acc_ref,
     low_of,
     end_of,
-    in_sems,
-    out_sems,
     piece_sems,
 ):
     lane = lane_ref[0]
     columns = GROUP_HEADS * SLAB
 
-    def copy_in(z):
-        return pltpu.make_async_copy(slots_hbm.at[:, z], slots_ref.at[z], in_sems.at[z])
-
     pieces = [
         pltpu.make_async_copy(piece, kv_ref.at[:, (lane - back) & (N_X - 1)], piece_sems.at[back])
         for back, piece in enumerate((piece_0, piece_1, piece_2, piece_3))
     ]
 
-    for z in range(N_Z):
-        copy_in(z).start()
     for piece in pieces:
         piece.start()
 
@@ -188,8 +179,7 @@
         tops_ref[z] = jnp.full((8, columns), MASKED, jnp.float32)
         sums_ref[z] = jnp.zeros((8, columns), jnp.float32)
         acc_ref[z] = jnp.zeros((HEAD_SIZE, columns), jnp.float32)
-        copy_in(z).wait()
-        slots = slots_ref[z].reshape(N_DP * Q_ROWS, WIDE)
+        slots = slots_ref[:, z].reshape(N_DP * Q_ROWS, WIDE)
         query_t = contract(slots, select_ref[z], 0, 0).astype(jnp.bfloat16)
         query_ref[z, :, : columns // 2] = query_t[:HEAD_SIZE]
         query_ref[z, :, columns // 2 :] = query_t[HEAD_SIZE:]
@@ -247,12 +237,7 @@
             [attended_t[:, : columns // 2], attended_t[:, columns // 2 :]], axis=0
         )
         back = contract(select_ref[z], attended_t, 1, 1).astype(jnp.bfloat16)
-        out_ref[z] = back.reshape(N_DP, Q_ROWS, WIDE)
-        copy_slab(out_ref, out_hbm, out_sems, z).start()
-
-    @pl.loop(0, N_Z)
-    def _(z):
-        copy_slab(out_ref, out_hbm, out_sems, z).wait()
+        out_ref[:, z] = back.reshape(N_DP, Q_ROWS, WIDE)
 
 
 def unpack_kernel(targets_ref, slots_ref, out_hbm, out_ref, sems):
@@ -344,14 +329,12 @@
         attend_kernel,
         "attend",
         [(q_blocks, half)],
-        [S, S, V] + [pl.ANY] * (1 + N_X),
+        [S, S, V, V] + [pl.ANY] * N_X,
         4 * 10**9,
         5 * 10**6,
         3 * 10**6,
         [
             V((N_Z, N_X, 2 * SLAB, HEAD_SIZE), half),
-            V((N_Z, N_DP, Q_ROWS, WIDE), half),
-            V((N_Z, N_DP, Q_ROWS, WIDE), half),
             V((N_Z, N_DP * Q_ROWS, HEAD_PAIRS * SLAB), half),
             V((N_Z, HEAD_SIZE, columns), half),
             V((MAX_ITEMS, PAIR, columns), f32),
@@ -360,12 +343,9 @@
             V((N_Z, HEAD_SIZE, columns), f32),
             S((N_Z,), whole),
             S((N_Z,), whole),
-            pltpu.SemaphoreType.DMA((N_Z,)),
-            pltpu.SemaphoreType.DMA((N_Z,)),
             pltpu.SemaphoreType.DMA((N_X,)),
         ],
         40 * 1024 * 1024,
-        pl.ANY,
     )(doc_lengths.reshape(DOCS), lane, code, q_slots, *pieces)
     out_slots = exchange(out_sent)
     (out,) = call(

time: 164 us -> 163 us (level)
  no operation moved by 1% of the time
where the time goes in v7:
time: 163 us
  waiting for transfers between devices  61.9 us (38%)
  blocking collectives  47.9 us (29%)
  starting transfers between devices  33.2 us (20%)
  Pallas kernels  17.3 us (11%)
  local copies, waits for them, and re-layouts  1.89 us (1%)
    all_to_all x1, blocking collectives, exchange(): lax.all_to_all(flat, EXCHANGE, split_axis=0, concat_axis=0, tiled=True)  47.9 us
    all_to_all x2, waiting for transfers between devices, exchange(): lax.all_to_all(flat, EXCHANGE, split_axis=0, concat_axis=0, tiled=True)  38.2 us
    all_to_all x2, starting transfers between devices, exchange(): lax.all_to_all(flat, EXCHANGE, split_axis=0, concat_axis=0, tiled=True)  23.9 us
    ppermute x3, waiting for transfers between devices, local(): lax.ppermute(kv_placed, 'x', [(x, (x + back) % N_X) for x in range(N_X)])  23.6 us
    pallas_call x1, Pallas kernels, local(): call(attend_kernel, 'attend', [(q_blocks, half)], [S, S, V, V] + [pl.ANY]...  12.3 us
    ppermute x3, starting transfers between devices, local(): lax.ppermute(kv_placed, 'x', [(x, (x + back) % N_X) for x in range(N_X)])  9.33 us
  transfers between devices with their start and end apart: 5, of which 5 were waited for; matrix products, arithmetic and copies ran while one was open for 1% of the time, Pallas kernels for 1%

profile of v7, /device:TPU:1, one launch (start us, length us, event | category | flops | bytes accessed | tf_op | source)
XLA Modules:
  0.0 163.0 jit_solution(16091242462099556651)
XLA Ops:
  0.0 2.4 %pack_kv.1 = bf16[16,8,16,256]{3,2,1,0:T(8,128)(2,1)} custom-call(s32[1,1,128]{2,1,0:T(1,128)} %code_ref.1, s32[1,1,128]{2,1,0:T(1,128)} %table_ref.1, bf16[128,1024]{1,0:T(8,128)(2,1)} %key_ref.1, bf16[128,1024]{1,0:T(8,128)(2,1)} %value_ref.1), custom_call_target="tpu_custom_call" | custom-call | flops 200000000 | bytes 2000000 | tf_op jit(solution)/shard_map/pack_kv/pallas_call | solution.py:284
  2.4 18.4 %all-to-all-start = ((bf16[128,16,256]{2,1,0:T(8,128)(2,1)}), bf16[128,16,256]{2,1,0:T(8,128)(2,1)S(1)}, u32[]{:S(2)}, u32[]{:S(2)}) async-start(bf16[128,16,256]{2,1,0:T(8,128)(2,1)} %bitcast.17), calls=%async_computation | async-start | bytes 2097152 | tf_op jit(solution)/shard_map/all_to_all | solution.py:274
  20.9 0.5 broadcast.33
  21.4 0.0 copy-done.4
  21.4 0.7 reduce.3
  22.1 0.1 reshape.87
  22.2 0.1 add_select_fusion
  22.3 0.1 select_n.15.targets_ref
  22.4 0.0 copy-done.1
  22.4 0.6 pack_q.1
  23.0 1.1 copy-done
  24.1 28.8 %all-to-all-done = bf16[128,16,256]{2,1,0:T(8,128)(2,1)S(1)} async-done(((bf16[128,16,256]{2,1,0:T(8,128)(2,1)}), bf16[128,16,256]{2,1,0:T(8,128)(2,1)S(1)}, u32[]{:S(2)}, u32[]{:S(2)}) %all-to-all-start) | async-done | bytes 1048608 | tf_op jit(solution)/shard_map/all_to_all | solution.py:274
  52.9 5.5 %all-to-all-start.1 = ((bf16[128,24,256]{2,1,0:T(8,128)(2,1)}), bf16[128,24,256]{2,1,0:T(8,128)(2,1)S(1)}, u32[]{:S(2)}, u32[]{:S(2)}) async-start(bf16[128,24,256]{2,1,0:T(8,128)(2,1)} %bitcast.12), calls=%async_computation.1 | async-start | bytes 3145728 | tf_op jit(solution)/shard_map/all_to_all | solution.py:274
  58.4 0.5 place_kv.1
  58.9 4.4 %collective-permute-start.2 = (bf16[8,256,128]{2,1,0:T(8,128)(2,1)S(1)}, bf16[8,256,128]{2,1,0:T(8,128)(2,1)S(1)}, u32[]{:S(2)}, u32[]{:S(2)}) collective-permute-start(bf16[8,256,128]{2,1,0:T(8,128)(2,1)S(1)} %get-tuple-element.14.piece_0), channel_id=1, source_target_pairs={{0,3},{1,0},{2,1},{3,2},{4,7},{5,4},{6,5},{7,6},{8,11},{9,8},{10,9... | collective-permute-start | bytes 1572872 | tf_op jit(solution)/shard_map/ppermute | solution.py:324
  63.3 2.4 %collective-permute-start.1 = (bf16[8,256,128]{2,1,0:T(8,128)(2,1)S(1)}, bf16[8,256,128]{2,1,0:T(8,128)(2,1)S(1)}, u32[]{:S(2)}, u32[]{:S(2)}) collective-permute-start(bf16[8,256,128]{2,1,0:T(8,128)(2,1)S(1)} %get-tuple-element.14.piece_0), channel_id=1, source_target_pairs={{0,2},{1,3},{2,0},{3,1},{4,6},{5,7},{6,4},{7,5},{8,10},{9,11},{10,... | collective-permute-start | bytes 1572872 | tf_op jit(solution)/shard_map/ppermute | solution.py:324
  65.7 2.5 %collective-permute-start = (bf16[8,256,128]{2,1,0:T(8,128)(2,1)S(1)}, bf16[8,256,128]{2,1,0:T(8,128)(2,1)}, u32[]{:S(2)}, u32[]{:S(2)}) collective-permute-start(bf16[8,256,128]{2,1,0:T(8,128)(2,1)S(1)} %get-tuple-element.14.piece_0), channel_id=1, source_target_pairs={{0,1},{1,2},{2,3},{3,0},{4,5},{5,6},{6,7},{7,4},{8,9},{9,10},{10,1... | collective-permute-start | bytes 1572872 | tf_op jit(solution)/shard_map/ppermute | solution.py:324
  68.3 6.4 %collective-permute-done.2.piece_3 = bf16[8,256,128]{2,1,0:T(8,128)(2,1)S(1)} collective-permute-done((bf16[8,256,128]{2,1,0:T(8,128)(2,1)S(1)}, bf16[8,256,128]{2,1,0:T(8,128)(2,1)S(1)}, u32[]{:S(2)}, u32[]{:S(2)}) %collective-permute-start.2) | collective-permute-done | bytes 524320 | tf_op jit(solution)/shard_map/ppermute | solution.py:324
  74.6 4.5 %collective-permute-done.1.piece_2 = bf16[8,256,128]{2,1,0:T(8,128)(2,1)S(1)} collective-permute-done((bf16[8,256,128]{2,1,0:T(8,128)(2,1)S(1)}, bf16[8,256,128]{2,1,0:T(8,128)(2,1)S(1)}, u32[]{:S(2)}, u32[]{:S(2)}) %collective-permute-start.1) | collective-permute-done | bytes 524320 | tf_op jit(solution)/shard_map/ppermute | solution.py:324
  79.2 12.7 %collective-permute-done.piece_1 = bf16[8,256,128]{2,1,0:T(8,128)(2,1)} collective-permute-done((bf16[8,256,128]{2,1,0:T(8,128)(2,1)S(1)}, bf16[8,256,128]{2,1,0:T(8,128)(2,1)}, u32[]{:S(2)}, u32[]{:S(2)}) %collective-permute-start) | collective-permute-done | bytes 524320 | tf_op jit(solution)/shard_map/ppermute | solution.py:324
  91.9 9.4 %all-to-all-done.1 = bf16[128,24,256]{2,1,0:T(8,128)(2,1)S(1)} async-done(((bf16[128,24,256]{2,1,0:T(8,128)(2,1)}), bf16[128,24,256]{2,1,0:T(8,128)(2,1)S(1)}, u32[]{:S(2)}, u32[]{:S(2)}) %all-to-all-start.1) | async-done | bytes 1572896 | tf_op jit(solution)/shard_map/all_to_all | solution.py:274
  101.3 12.3 %attend.1 = bf16[16,8,24,256]{3,2,1,0:T(8,128)(2,1)S(1)} custom-call(s32[8]{0:T(128)S(1)} %bitcast.16, s32[1]{0:T(128)} %bitcast.4.lane_ref, s32[8,128]{1,0:T(8,128)S(1)} %get-tuple-element.12.code_ref, bf16[16,8,24,256]{3,2,1,0:T(8,128)(2,1)S(1)} %bitcast.11, bf16[8,256,128]{2,1,0:T(8,128)(2,1)S(1)} %get-tuple-element.14.piece_0, ...), custom_call_target="tpu_custom_call" | custom-call | flops 4000000000 | bytes 5000000 | tf_op jit(solution)/shard_map/attend/pallas_call | solution.py:328
  113.6 47.9 %all_to_all.15 = bf16[128,24,256]{2,1,0:T(8,128)(2,1)S(1)} all-to-all(bf16[128,24,256]{2,1,0:T(8,128)(2,1)S(1)} %bitcast.13), channel_id=1, replica_groups=mesh['y'=8,'core'=2,'z'=8,'x'=4] {'y','core','z'}, dimensions={0} | all-to-all | bytes 3145728 | tf_op jit(solution)/shard_map/all_to_all | solution.py:274
  161.5 1.5 unpack.1
  (9 shorter events, 0.0 us)
Async XLA Ops:
  0.0 22.4 %copy-start.1 = (s32[1,1,128]{2,1,0:T(1,128)S(1)}, s32[1,1,128]{2,1,0:T(1,128)}, u32[]{:S(2)}) copy-start(s32[1,1,128]{2,1,0:T(1,128)} %code_ref.1) | copy-start | bytes 1540
  0.0 21.4 %copy-start.4 = (s32[1,1,192]{2,1,0:T(1,128)S(1)}, s32[1,1,192]{2,1,0:T(1,128)}, u32[]{:S(2)}) copy-start(s32[1,1,192]{2,1,0:T(1,128)} %param.12) | copy-start | bytes 2308
  0.0 22.4 %copy-start.2 = (bf16[128,4096]{1,0:T(8,128)(2,1)S(1)}, bf16[128,4096]{1,0:T(8,128)(2,1)}, u32[]{:S(2)}) copy-start(bf16[128,4096]{1,0:T(8,128)(2,1)} %query_ref.1) | copy-start | bytes 3145732
  2.4 50.5 %all-to-all-start = ((bf16[128,16,256]{2,1,0:T(8,128)(2,1)}), bf16[128,16,256]{2,1,0:T(8,128)(2,1)S(1)}, u32[]{:S(2)}, u32[]{:S(2)}) async-start(bf16[128,16,256]{2,1,0:T(8,128)(2,1)} %bitcast.17), calls=%async_computation | async-start | bytes 2097152 | tf_op jit(solution)/shard_map/all_to_all | solution.py:274
  23.0 1.2 copy-start
  52.9 48.4 %copy-start.3 = (s32[1,1,8]{2,1,0:T(1,128)S(1)}, s32[1,1,8]{2,1,0:T(1,128)}, u32[]{:S(2)}) copy-start(s32[1,1,8]{2,1,0:T(1,128)} %param.11) | copy-start | bytes 100
  52.9 48.4 %all-to-all-start.1 = ((bf16[128,24,256]{2,1,0:T(8,128)(2,1)}), bf16[128,24,256]{2,1,0:T(8,128)(2,1)S(1)}, u32[]{:S(2)}, u32[]{:S(2)}) async-start(bf16[128,24,256]{2,1,0:T(8,128)(2,1)} %bitcast.12), calls=%async_computation.1 | async-start | bytes 3145728 | tf_op jit(solution)/shard_map/all_to_all | solution.py:274
  58.9 15.7 %collective-permute-start.2 = (bf16[8,256,128]{2,1,0:T(8,128)(2,1)S(1)}, bf16[8,256,128]{2,1,0:T(8,128)(2,1)S(1)}, u32[]{:S(2)}, u32[]{:S(2)}) collective-permute-start(bf16[8,256,128]{2,1,0:T(8,128)(2,1)S(1)} %get-tuple-element.14.piece_0), channel_id=1, source_target_pairs={{0,3},{1,0},{2,1},{3,2},{4,7},{5,4},{6,5},{7,6},{8,11},{9,8},{10,9... | collective-permute-start | bytes 1572872 | tf_op jit(solution)/shard_map/ppermute | solution.py:324
  63.3 15.9 %collective-permute-start.1 = (bf16[8,256,128]{2,1,0:T(8,128)(2,1)S(1)}, bf16[8,256,128]{2,1,0:T(8,128)(2,1)S(1)}, u32[]{:S(2)}, u32[]{:S(2)}) collective-permute-start(bf16[8,256,128]{2,1,0:T(8,128)(2,1)S(1)} %get-tuple-element.14.piece_0), channel_id=1, source_target_pairs={{0,2},{1,3},{2,0},{3,1},{4,6},{5,7},{6,4},{7,5},{8,10},{9,11},{10,... | collective-permute-start | bytes 1572872 | tf_op jit(solution)/shard_map/ppermute | solution.py:324
  65.7 26.1 %collective-permute-start = (bf16[8,256,128]{2,1,0:T(8,128)(2,1)S(1)}, bf16[8,256,128]{2,1,0:T(8,128)(2,1)}, u32[]{:S(2)}, u32[]{:S(2)}) collective-permute-start(bf16[8,256,128]{2,1,0:T(8,128)(2,1)S(1)} %get-tuple-element.14.piece_0), channel_id=1, source_target_pairs={{0,1},{1,2},{2,3},{3,0},{4,5},{5,6},{6,7},{7,4},{8,9},{9,10},{10,1... | collective-permute-start | bytes 1572872 | tf_op jit(solution)/shard_map/ppermute | solution.py:324
